TPU v7x, 128 devices: a whole 4x4x4 slice. The times are simulated.
128 devices in a mesh: dp: 16 (over y, x_lo, core), expert: 8 (over z, x_hi).
Axes of the slice: x: 4 (x_hi: 2, x_lo: 2; x = x_hi * 2 + x_lo), y: 4, z: 4, core: 2. Of those that a mesh axis runs over, the one named last changes fastest.
Arguments:
- tokens: bfloat16 [2, 16, 1024, 1024], P(None, 'dp', 'expert'), may hold values from -6 to 6
- cotangent: bfloat16 [2, 16, 1024, 1024], P(None, 'dp', 'expert'), may hold values from -6 to 6
- routes: int32 [2, 16, 1024, 8], P(None, 'dp', 'expert'), may hold values from 0 to 31, all different within a row; in each aligned block of 128 rows (0 to 127, 128 to 255, ..., all dimensions but the last counted through in order) at most 48 rows name the same one
- doc_lengths: int32 [2, 16, 6], P(None, 'dp'), may hold values from 1 to 512, 1024 in all within a row
- valid: int32 [2, 16, 1024], P(None, 'dp', 'expert'), may hold values 0 or 1
- attn_gain: bfloat16 [1024], P(('dp', 'expert')), may hold values from 0.25 to 1.75
- w_query: bfloat16 [1024, 1024], P(('dp', 'expert')), may hold values from -0.1875 to 0.1875
- w_key: bfloat16 [1024, 512], P(('dp', 'expert')), may hold values from -0.1875 to 0.1875
- w_value: bfloat16 [1024, 512], P(('dp', 'expert')), may hold values from -0.1875 to 0.1875
- query_gain: bfloat16 [64], replicated, may hold values from 0.25 to 1.75
- key_gain: bfloat16 [64], replicated, may hold values from 0.25 to 1.75
- w_out: bfloat16 [1024, 1024], P(('dp', 'expert')), may hold values from -1.5 to 1.5
- ffn_gain: bfloat16 [1024], P(('dp', 'expert')), may hold values from 0.25 to 1.75
- w_router: bfloat16 [1024, 32], P(('dp', 'expert')), may hold values from -0.09375 to 0.09375
- w_gate: bfloat16 [32, 1024, 512], P('expert', 'dp'), may hold values from -0.1875 to 0.1875
- w_up: bfloat16 [32, 1024, 512], P('expert', 'dp'), may hold values from -0.1875 to 0.1875
- w_down: bfloat16 [32, 512, 1024], P('expert', 'dp'), may hold values from -1 to 1
Outputs:
- output: bfloat16 [2, 16, 1024, 1024], P(None, 'dp', 'expert')
- tokens_grad: bfloat16 [2, 16, 1024, 1024], P(None, 'dp', 'expert')
- attn_gain_grad: float32 [1024], P(('dp', 'expert'))
- w_query_grad: float32 [1024, 1024], P(('dp', 'expert'))
- w_key_grad: float32 [1024, 512], P(('dp', 'expert'))
- w_value_grad: float32 [1024, 512], P(('dp', 'expert'))
- query_gain_grad: float32 [64], replicated
- key_gain_grad: float32 [64], replicated
- w_out_grad: float32 [1024, 1024], P(('dp', 'expert'))
- ffn_gain_grad: float32 [1024], P(('dp', 'expert'))
- w_router_grad: float32 [1024, 32], P(('dp', 'expert'))
- w_gate_grad: float32 [32, 1024, 512], P('expert', 'dp')
- w_up_grad: float32 [32, 1024, 512], P('expert', 'dp')
- w_down_grad: float32 [32, 512, 1024], P('expert', 'dp')
Inputs may be any that keep to these rules, and one draw needn't show every extreme that they name: `routes`: in each aligned block of 128 positions of a sequence, no expert is named more than 48 times; the 8 experts of a token differ. `doc_lengths`: the 6 lengths of a sequence sum to 1024; the largest is exactly half of 1024.
All inputs are finite; a program needn't handle non-finite values. No bound on the sum of `valid` on one device may be relied on, other than what follows from the above.
Results may differ from a plain program's by a relative error of at most 0.02.
Values may be sent and summed in bfloat16 or wider, within the bound.
No kernel may reach another device: no remote copies, remote signals or barrier semaphores. Data moves between devices by JAX's collectives and lax.ppermute only.
A program may use at most 192 MiB of HBM per device.

v0:
```python
import math

import jax
import jax.numpy as jnp
from jax import lax
from jax.sharding import PartitionSpec as P

WINDOW = 256


EPSILON = 1e-06
ROPE_BASE = 10000.0


def passed_along(value, axis, steps):
    count = lax.axis_size(axis)
    initial, last = (max(0, -steps), min(count, count - steps))
    return lax.ppermute(value, axis, [(source, source + steps) for source in range(initial, last)])


def rms_scale(values):
    return lax.rsqrt(jnp.mean(values * values, axis=-1, keepdims=True) + EPSILON)


def rope_tables(positions, head_size):
    half_size = head_size // 2
    frequency = jnp.exp(
        -math.log(ROPE_BASE) * (2.0 * jnp.arange(half_size, dtype=jnp.float32) / head_size)
    )
    angles = positions.astype(jnp.float32)[:, None] * frequency[None, :]
    angles = jnp.concatenate([angles, angles], axis=-1)
    return (jnp.cos(angles), jnp.sin(angles))


def rotate(values, cosine, sine):
    half_size = values.shape[-1] // 2
    turned = jnp.concatenate([-values[..., half_size:], values[..., :half_size]], axis=-1)
    return values * cosine[:, None, :] + turned * sine[:, None, :]


def rotate_back(upstream, cosine, sine):
    half_size = upstream.shape[-1] // 2
    scaled = upstream * sine[:, None, :]
    turned = jnp.concatenate([scaled[..., half_size:], -scaled[..., :half_size]], axis=-1)
    return upstream * cosine[:, None, :] + turned


def norm_back(upstream, values, scaling):
    return scaling * upstream - values * (scaling * scaling * scaling) * jnp.mean(
        upstream * values, axis=-1, keepdims=True
    )


def product_tn(left_side, right_side):
    return lax.dot_general(
        left_side, right_side, (((0,), (0,)), ((), ())), preferred_element_type=jnp.float32
    )


def product_nt(left_side, right_side):
    return lax.dot_general(
        left_side, right_side, (((1,), (1,)), ((), ())), preferred_element_type=jnp.float32
    )


def accumulate(previous, addend):
    if previous is None:
        return addend
    return previous + addend


def body(
    tokens,
    cotangent,
    routes,
    doc_lengths,
    valid,
    attn_gain,
    w_query,
    w_key,
    w_value,
    query_gain,
    key_gain,
    w_out,
    ffn_gain,
    w_router,
    w_gate,
    w_up,
    w_down,
):
    bf16 = jnp.bfloat16
    f32 = jnp.float32
    micro_count = tokens.shape[0]
    tok_rows = tokens.shape[2]
    model_width = tokens.shape[3]
    head_size = query_gain.shape[0]
    q_width = w_query.shape[1]
    kv_width = w_key.shape[1]
    kv_heads = kv_width // head_size
    q_heads = q_width // head_size
    group_size = q_heads // kv_heads
    top_count = routes.shape[3]
    expert_count = w_router.shape[1]
    local_count = w_gate.shape[0]
    expert_devices = lax.axis_size("expert")
    capacity = tok_rows * top_count * 3 // (2 * expert_count)
    reach_back = (WINDOW + tok_rows - 2) // tok_rows
    key_rows = tok_rows * (reach_back + 1)
    score_scale = 1.0 / math.sqrt(head_size)
    q_gain = query_gain.astype(f32)
    k_gain = key_gain.astype(f32)

    def fetch_all():
        dense_set = (
            lax.all_gather(attn_gain, ("dp", "expert"), axis=0, tiled=True),
            lax.all_gather(w_query, ("dp", "expert"), axis=0, tiled=True),
            lax.all_gather(w_key, ("dp", "expert"), axis=0, tiled=True),
            lax.all_gather(w_value, ("dp", "expert"), axis=0, tiled=True),
            lax.all_gather(w_out, ("dp", "expert"), axis=0, tiled=True),
            lax.all_gather(ffn_gain, ("dp", "expert"), axis=0, tiled=True),
            lax.all_gather(w_router, ("dp", "expert"), axis=0, tiled=True),
        )
        expert_set = (
            lax.all_gather(w_gate, "dp", axis=1, tiled=True),
            lax.all_gather(w_up, "dp", axis=1, tiled=True),
            lax.all_gather(w_down, "dp", axis=1, tiled=True),
        )
        return (dense_set, expert_set)

    def weights_now():
        return fetch_all()

    def to_experts(slot_rows):
        shaped = slot_rows.reshape(expert_devices, local_count, capacity, model_width)
        arrived = lax.all_to_all(shaped, "expert", split_axis=0, concat_axis=2, tiled=True)
        return arrived.reshape(local_count, expert_devices * capacity, model_width)

    expert_index = lax.axis_index("expert")
    q_pos = expert_index * tok_rows + jnp.arange(tok_rows, dtype=jnp.int32)
    k_pos = (expert_index - reach_back) * tok_rows + jnp.arange(key_rows, dtype=jnp.int32)
    cosine, sine = rope_tables(q_pos, head_size)
    expert_ids = jnp.arange(expert_count, dtype=jnp.int32)
    stored = []
    outputs = []
    for micro_step in range(micro_count):
        dense_set, expert_set = weights_now()
        gain_attn = dense_set[0].astype(f32)
        query_full, key_full, value_full, out_full = (
            dense_set[1],
            dense_set[2],
            dense_set[3],
            dense_set[4],
        )
        gain_ffn = dense_set[5].astype(f32)
        router_full = dense_set[6]
        gate_full, up_full, down_full = expert_set
        x_float = tokens[micro_step, 0].astype(f32)
        attn_scale = rms_scale(x_float)
        normed = (x_float * attn_scale * gain_attn).astype(bf16)
        query = jnp.dot(normed, query_full, preferred_element_type=f32).reshape(
            tok_rows, q_heads, head_size
        )
        key_pre = jnp.dot(normed, key_full, preferred_element_type=f32).reshape(
            tok_rows, kv_heads, head_size
        )
        value_low = jnp.dot(normed, value_full, preferred_element_type=f32).astype(bf16)
        query_scale = rms_scale(query)
        key_scale = rms_scale(key_pre)
        query_rot = rotate(query * query_scale * q_gain, cosine, sine).astype(bf16)
        key_rot = (
            rotate(key_pre * key_scale * k_gain, cosine, sine)
            .astype(bf16)
            .reshape(tok_rows, kv_width)
        )
        key_parts = [key_rot]
        value_parts = [value_low]
        for distance in range(1, reach_back + 1):
            key_prev, value_prev = passed_along((key_rot, value_low), "expert", distance)
            key_parts = [key_prev] + key_parts
            value_parts = [value_prev] + value_parts
        keys_all = jnp.concatenate(key_parts, axis=0).reshape(key_rows, kv_heads, head_size)
        values_all = jnp.concatenate(value_parts, axis=0).reshape(key_rows, kv_heads, head_size)
        bounds = jnp.cumsum(doc_lengths[micro_step, 0])
        q_doc = jnp.sum((q_pos[:, None] >= bounds[None, :]).astype(jnp.int32), axis=1)
        k_doc = jnp.sum((k_pos[:, None] >= bounds[None, :]).astype(jnp.int32), axis=1)
        offset = q_pos[:, None] - k_pos[None, :]
        visible = (
            (k_pos[None, :] >= 0)
            & (q_doc[:, None] == k_doc[None, :])
            & (offset >= 0)
            & (offset < WINDOW)
        )
        query_group = query_rot.reshape(tok_rows, kv_heads, group_size, head_size)
        scores = (
            jnp.einsum("tkgd,skd->kgts", query_group, keys_all, preferred_element_type=f32)
            * score_scale
        )
        scores = jnp.where(visible[None, None], scores, -1e30)
        row_peak = jnp.max(scores, axis=-1, keepdims=True)
        exp_scores = jnp.exp(scores - row_peak)
        row_total = jnp.sum(exp_scores, axis=-1, keepdims=True)
        attn_probs = exp_scores / row_total
        log_total = row_peak + jnp.log(row_total)
        attended = (
            jnp.einsum(
                "kgts,skd->tkgd", attn_probs.astype(bf16), values_all, preferred_element_type=f32
            )
            .reshape(tok_rows, q_width)
            .astype(bf16)
        )
        middle = x_float + jnp.dot(attended, out_full, preferred_element_type=f32)
        ffn_scale = rms_scale(middle)
        moe_in = (middle * ffn_scale * gain_ffn).astype(bf16)
        logits = jnp.dot(moe_in, router_full, preferred_element_type=f32)
        route_ids = routes[micro_step, 0]
        one_hot = (route_ids[:, :, None] == expert_ids[None, None, :]).astype(f32)
        chosen = jnp.sum(one_hot * logits[:, None, :], axis=-1)
        gate_probs = jax.nn.softmax(chosen, axis=-1)
        flat_hot = one_hot.reshape(tok_rows * top_count, expert_count).astype(jnp.int32)
        slot_rank = jnp.sum((jnp.cumsum(flat_hot, axis=0) - 1) * flat_hot, axis=1)
        slot_ids = route_ids.reshape(-1) * capacity + slot_rank
        outgoing = (
            jnp.zeros((expert_count * capacity, model_width), bf16)
            .at[slot_ids]
            .set(jnp.repeat(moe_in, top_count, axis=0))
        )
        arrived = to_experts(outgoing)
        gate_pre = jnp.einsum("ecd,edf->ecf", arrived, gate_full, preferred_element_type=f32)
        up_pre = jnp.einsum("ecd,edf->ecf", arrived, up_full, preferred_element_type=f32)
        hidden = (jax.nn.silu(gate_pre) * up_pre).astype(bf16)
        expert_out = jnp.einsum(
            "ecf,efd->ecd", hidden, down_full, preferred_element_type=f32
        ).astype(bf16)
        returned = lax.all_to_all(
            expert_out.reshape(1, local_count, expert_devices * capacity, model_width),
            "expert",
            split_axis=2,
            concat_axis=0,
            tiled=True,
        )
        returned = returned.reshape(expert_count * capacity, model_width)
        picked = jnp.take(returned, slot_ids, axis=0).reshape(tok_rows, top_count, model_width)
        mixed = middle + jnp.sum(gate_probs[:, :, None] * picked.astype(f32), axis=1)
        outputs.append(mixed.astype(bf16))
        stored.append(
            (
                x_float,
                attn_scale,
                normed,
                query,
                query_scale,
                key_pre,
                key_scale,
                query_group,
                keys_all,
                values_all,
                visible,
                log_total,
                attended,
                middle,
                ffn_scale,
                moe_in,
                one_hot,
                gate_probs,
                slot_ids,
                picked,
                arrived,
                gate_pre,
                up_pre,
                hidden,
            )
        )
    acc_attn_gain = None
    acc_query = None
    acc_key = None
    acc_value = None
    acc_query_gain = None
    acc_key_gain = None
    acc_out = None
    acc_ffn_gain = None
    acc_router = None
    acc_gate = None
    acc_up = None
    acc_down = None
    token_grads = []
    for micro_step in reversed(range(micro_count)):
        (
            x_float,
            attn_scale,
            normed,
            query,
            query_scale,
            key_pre,
            key_scale,
            query_group,
            keys_all,
            values_all,
            visible,
            log_total,
            attended,
            middle,
            ffn_scale,
            moe_in,
            one_hot,
            gate_probs,
            slot_ids,
            picked,
            arrived,
            gate_pre,
            up_pre,
            hidden,
        ) = stored[micro_step]
        dense_set, expert_set = weights_now()
        gain_attn = dense_set[0].astype(f32)
        query_full, key_full, value_full, out_full = (
            dense_set[1],
            dense_set[2],
            dense_set[3],
            dense_set[4],
        )
        gain_ffn = dense_set[5].astype(f32)
        router_full = dense_set[6]
        gate_full, up_full, down_full = expert_set
        out_seed = cotangent[micro_step, 0].astype(f32) * valid[micro_step, 0][:, None].astype(f32)
        out_rows = (gate_probs[:, :, None] * out_seed[:, None, :]).astype(bf16)
        gate_grad = jnp.sum(out_seed[:, None, :] * picked.astype(f32), axis=-1)
        chosen_grad = gate_probs * (
            gate_grad - jnp.sum(gate_probs * gate_grad, axis=-1, keepdims=True)
        )
        logit_grad = jnp.sum(one_hot * chosen_grad[:, :, None], axis=1).astype(bf16)
        acc_router = accumulate(acc_router, product_tn(moe_in, logit_grad))
        moe_grad = product_nt(logit_grad, router_full)
        outgoing = (
            jnp.zeros((expert_count * capacity, model_width), bf16)
            .at[slot_ids]
            .set(out_rows.reshape(tok_rows * top_count, model_width))
        )
        arrived_grad = to_experts(outgoing)
        hidden_grad = jnp.einsum(
            "ecd,efd->ecf", arrived_grad, down_full, preferred_element_type=f32
        )
        acc_down = accumulate(
            acc_down, jnp.einsum("ecf,ecd->efd", hidden, arrived_grad, preferred_element_type=f32)
        )
        sigma = jax.nn.sigmoid(gate_pre)
        gate_act = gate_pre * sigma
        gate_low = (hidden_grad * up_pre * sigma * (1.0 + gate_pre * (1.0 - sigma))).astype(bf16)
        up_low = (hidden_grad * gate_act).astype(bf16)
        acc_gate = accumulate(
            acc_gate, jnp.einsum("ecd,ecf->edf", arrived, gate_low, preferred_element_type=f32)
        )
        acc_up = accumulate(
            acc_up, jnp.einsum("ecd,ecf->edf", arrived, up_low, preferred_element_type=f32)
        )
        row_grad = jnp.einsum(
            "ecf,edf->ecd", gate_low, gate_full, preferred_element_type=f32
        ) + jnp.einsum("ecf,edf->ecd", up_low, up_full, preferred_element_type=f32)
        row_back = lax.all_to_all(
            row_grad.reshape(1, local_count, expert_devices * capacity, model_width).astype(
                jnp.bfloat16
            ),
            "expert",
            split_axis=2,
            concat_axis=0,
            tiled=True,
        ).astype(jnp.float32)
        row_back = row_back.reshape(expert_count * capacity, model_width)
        moe_grad = moe_grad + jnp.sum(
            jnp.take(row_back, slot_ids, axis=0).reshape(tok_rows, top_count, model_width), axis=1
        )
        acc_ffn_gain = accumulate(acc_ffn_gain, jnp.sum(moe_grad * middle * ffn_scale, axis=0))
        mid_grad = out_seed + norm_back(moe_grad * gain_ffn, middle, ffn_scale)
        branch_low = mid_grad.astype(bf16)
        acc_out = accumulate(acc_out, product_tn(attended, branch_low))
        attended_grad = (
            product_nt(branch_low, out_full)
            .astype(bf16)
            .reshape(tok_rows, kv_heads, group_size, head_size)
        )
        scores = (
            jnp.einsum("tkgd,skd->kgts", query_group, keys_all, preferred_element_type=f32)
            * score_scale
        )
        scores = jnp.where(visible[None, None], scores, -1e30)
        attn_probs = jnp.where(visible[None, None], jnp.exp(scores - log_total), 0.0)
        prob_grad = jnp.einsum(
            "tkgd,skd->kgts", attended_grad, values_all, preferred_element_type=f32
        )
        inner = jnp.sum(attn_probs * prob_grad, axis=-1, keepdims=True)
        score_low = (score_scale * attn_probs * (prob_grad - inner)).astype(bf16)
        value_grad = jnp.einsum(
            "kgts,tkgd->skd", attn_probs.astype(bf16), attended_grad, preferred_element_type=f32
        ).reshape(key_rows, kv_width)
        query_rot_grad = jnp.einsum(
            "kgts,skd->tkgd", score_low, keys_all, preferred_element_type=f32
        ).reshape(tok_rows, q_heads, head_size)
        key_rot_grad = jnp.einsum(
            "kgts,tkgd->skd", score_low, query_group, preferred_element_type=f32
        ).reshape(key_rows, kv_width)
        start_local = reach_back * tok_rows
        key_local = key_rot_grad[start_local:]
        value_local = value_grad[start_local:]
        for distance in range(1, reach_back + 1):
            first_row = (reach_back - distance) * tok_rows
            key_ret, value_ret = (
                passed_along(
                    key_rot_grad[first_row : first_row + tok_rows].astype(jnp.bfloat16),
                    "expert",
                    -distance,
                ).astype(jnp.float32),
                passed_along(
                    value_grad[first_row : first_row + tok_rows].astype(jnp.bfloat16),
                    "expert",
                    -distance,
                ).astype(jnp.float32),
            )
            key_local = key_local + key_ret
            value_local = value_local + value_ret
        value_low_grad = value_local.astype(bf16)
        key_norm_grad = rotate_back(key_local.reshape(tok_rows, kv_heads, head_size), cosine, sine)
        acc_key_gain = accumulate(
            acc_key_gain, jnp.sum(key_norm_grad * key_pre * key_scale, axis=(0, 1))
        )
        key_low = (
            norm_back(key_norm_grad * k_gain, key_pre, key_scale)
            .reshape(tok_rows, kv_width)
            .astype(bf16)
        )
        query_norm_grad = rotate_back(query_rot_grad, cosine, sine)
        acc_query_gain = accumulate(
            acc_query_gain, jnp.sum(query_norm_grad * query * query_scale, axis=(0, 1))
        )
        query_low = (
            norm_back(query_norm_grad * q_gain, query, query_scale)
            .reshape(tok_rows, q_width)
            .astype(bf16)
        )
        acc_query = accumulate(acc_query, product_tn(normed, query_low))
        acc_key = accumulate(acc_key, product_tn(normed, key_low))
        acc_value = accumulate(acc_value, product_tn(normed, value_low_grad))
        normed_grad = (
            product_nt(query_low, query_full)
            + product_nt(key_low, key_full)
            + product_nt(value_low_grad, value_full)
        )
        acc_attn_gain = accumulate(
            acc_attn_gain, jnp.sum(normed_grad * x_float * attn_scale, axis=0)
        )
        token_grads = [
            (mid_grad + norm_back(normed_grad * gain_attn, x_float, attn_scale)).astype(bf16)
        ] + token_grads
    all_devices = lax.axis_size("dp") * lax.axis_size("expert")
    gain_rows = jnp.broadcast_to(
        jnp.concatenate([acc_query_gain, acc_key_gain])[None, :], (all_devices, 2 * head_size)
    )
    owned = (
        lax.psum_scatter(acc_attn_gain, ("dp", "expert"), scatter_dimension=0, tiled=True),
        lax.psum_scatter(acc_query, ("dp", "expert"), scatter_dimension=0, tiled=True),
        lax.psum_scatter(acc_key, ("dp", "expert"), scatter_dimension=0, tiled=True),
        lax.psum_scatter(acc_value, ("dp", "expert"), scatter_dimension=0, tiled=True),
        lax.psum_scatter(acc_out, ("dp", "expert"), scatter_dimension=0, tiled=True),
        lax.psum_scatter(acc_ffn_gain, ("dp", "expert"), scatter_dimension=0, tiled=True),
        lax.psum_scatter(acc_router, ("dp", "expert"), scatter_dimension=0, tiled=True),
        lax.psum_scatter(gain_rows, ("dp", "expert"), scatter_dimension=0, tiled=True),
    )
    expert_owned = (
        lax.psum_scatter(
            acc_gate.astype(jnp.bfloat16), "dp", scatter_dimension=1, tiled=True
        ).astype(jnp.float32),
        lax.psum_scatter(acc_up.astype(jnp.bfloat16), "dp", scatter_dimension=1, tiled=True).astype(
            jnp.float32
        ),
        lax.psum_scatter(
            acc_down.astype(jnp.bfloat16), "dp", scatter_dimension=1, tiled=True
        ).astype(jnp.float32),
    )
    output = jnp.stack(outputs)[:, None]
    tokens_grad = jnp.stack(token_grads)[:, None]
    return (
        output,
        tokens_grad,
        owned[0],
        owned[1],
        owned[2],
        owned[3],
        owned[7][0, :head_size],
        owned[7][0, head_size:],
        owned[4],
        owned[5],
        owned[6],
        expert_owned[0],
        expert_owned[1],
        expert_owned[2],
    )


def solution(mesh):
    return jax.shard_map(
        body,
        mesh=mesh,
        in_specs=(
            P(None, "dp", "expert", None),
            P(None, "dp", "expert", None),
            P(None, "dp", "expert", None),
            P(None, "dp", None),
            P(None, "dp", "expert"),
            P(("dp", "expert")),
            P(("dp", "expert"), None),
            P(("dp", "expert"), None),
            P(("dp", "expert"), None),
            P(),
            P(),
            P(("dp", "expert"), None),
            P(("dp", "expert")),
            P(("dp", "expert"), None),
            P("expert", "dp", None),
            P("expert", "dp", None),
            P("expert", "dp", None),
        ),
        out_specs=(
            P(None, "dp", "expert", None),
            P(None, "dp", "expert", None),
            P(("dp", "expert")),
            P(("dp", "expert"), None),
            P(("dp", "expert"), None),
            P(("dp", "expert"), None),
            P(),
            P(),
            P(("dp", "expert"), None),
            P(("dp", "expert")),
            P(("dp", "expert"), None),
            P("expert", "dp", None),
            P("expert", "dp", None),
            P("expert", "dp", None),
        ),
        check_vma=False,
    )
```

profile of v0, /device:TPU:0, one launch (start us, length us, event | category | flops | bytes accessed | tf_op | source)
XLA Modules:
  0.0 5038.4 jit_solution(11227345457085085712)
XLA Ops:
  19.3 68.2 %all-reduce.8 = (bf16[1024]{0:T(1024)(128)(2,1)S(1)}, bf16[1024]{0:T(1024)(128)(2,1)S(1)}) all-reduce(bf16[1024]{0:T(1024)(128)(2,1)S(1)} %dynamic-update-slice, bf16[1024]{0:T(1024)(128)(2,1)S(1)} %dynamic-update-slice.1), channel_id=1, replica_groups=mesh['dp'=16,'expert'=8] {'dp','expert'}, use_global_device_ids=true, to_apply=%add | all-reduce | flops 2048 | bytes 8192
  88.2 9.0 reduce-window.37
  99.7 204.3 %all-gather.8.cloned.1.call-done = bf16[1024,512]{1,0:T(8,128)(2,1)} async-done(((bf16[8,512]{1,0:T(8,128)(2,1)}), bf16[1024,512]{1,0:T(8,128)(2,1)}) %all-gather.8.cloned.1.call-update) | async-done | bytes 1048592 | tf_op jit(solution)/shard_map/all_gather | solution.py:118
  305.6 4.9 collective-permute-start.1
  313.8 284.9 %all-gather.10.cloned.1.call-done = bf16[1024,512]{1,0:T(8,128)(2,1)} async-done(((bf16[8,512]{1,0:T(8,128)(2,1)}), bf16[1024,512]{1,0:T(8,128)(2,1)}) %all-gather.10.cloned.1.call-update) | async-done | bytes 1048592 | tf_op jit(solution)/shard_map/all_gather | solution.py:117
  603.8 5.0 collective-permute-start.3
  612.0 286.5 %all-gather.12.cloned.1.call-done = bf16[1024,1024]{1,0:T(8,128)(2,1)} async-done(((bf16[8,1024]{1,0:T(8,128)(2,1)}), bf16[1024,1024]{1,0:T(8,128)(2,1)}) %all-gather.12.cloned.1.call-update) | async-done | bytes 2097168 | tf_op jit(solution)/shard_map/all_gather | solution.py:116
  909.5 291.3 %all-gather.14.cloned.1.call-done = bf16[1024,1024]{1,0:T(8,128)(2,1)} async-done(((bf16[8,1024]{1,0:T(8,128)(2,1)}), bf16[1024,1024]{1,0:T(8,128)(2,1)}) %all-gather.14.cloned.1.call-update) | async-done | bytes 2097168 | tf_op jit(solution)/shard_map/all_gather | solution.py:119
  1203.7 6.5 scatter_custom_fusion
  1210.2 66.6 %all_to_all.108 = bf16[8,4,48,1024]{3,2,1,0:T(8,128)(2,1)S(1)} all-to-all(bf16[8,4,48,1024]{3,2,1,0:T(8,128)(2,1)S(1)} %bitcast.549), channel_id=1, replica_groups=mesh['dp'=16,'expert'=8] {'expert'}, dimensions={0} | all-to-all | bytes 6291456 | tf_op jit(solution)/shard_map/all_to_all | solution.py:135
  1277.3 6.8 fusion.189
  1284.0 10.2 all-gather.18.cloned.1.call-done
  1294.2 7.2 multiply_convert_fusion.5
  1301.5 32.5 all-gather.20.cloned.1.call-done
  1334.0 4.5 convert_bitcast_fusion.3
  1338.5 4.1 copy.168
  1342.6 6.7 all-to-all-start.1
  1349.3 342.3 %all_gather.26 = bf16[1024,32]{1,0:T(8,128)(2,1)S(1)} all-gather(bf16[8,32]{1,0:T(8,128)(2,1)S(1)} %copy-done.185), channel_id=1, replica_groups=mesh['dp'=16,'expert'=8] {'dp','expert'}, dimensions={0}, use_global_device_ids=true | all-gather | bytes 66048 | tf_op jit(solution)/shard_map/all_gather | solution.py:121
  1700.2 5.4 gather_fusion
  1709.1 7.9 scatter_custom_fusion.2
  1717.1 4.5 all-to-all-start.4
  1723.0 15.7 reduce-window.40
  1743.7 7.9 all-to-all-done.4
  1755.6 5.0 multiply_convert_fusion.2
  1765.9 4.1 copy.185
  1770.0 4.6 all-to-all-start.5
  1775.5 5.3 collective-permute-start.5
  1780.8 3.4 collective-permute-start.4
  1791.5 11.4 collective-permute-done.5
  1802.8 5.3 collective-permute-done.4
  1814.1 5.6 copy.186
  1819.8 9.4 gather_fusion.2
  1829.2 5.2 bitcast_reduce_fusion.1
  1836.2 6.7 scatter_custom_fusion.1
  1842.9 37.9 all_to_all.109
  1886.4 3.6 multiply_convert_fusion.4
  1893.0 4.1 copy.179
  1897.0 4.2 all-to-all-start.3
  1902.5 28.3 all-to-all-done.3
  1935.4 5.4 gather_fusion.1
  1943.7 7.0 scatter_custom_fusion.3
  1950.7 34.0 all_to_all.110
  1995.7 4.2 copy.195
  1999.9 4.6 all-to-all-start.7
  2007.9 5.7 fusion.198
  2013.7 20.9 all-to-all-done.7
  2034.6 5.6 copy.196
  2040.3 9.6 gather_fusion.3
  2049.9 4.6 bitcast_reduce_fusion
  2089.4 8.4 add_convert_fusion
  2099.6 3.9 fusion.197
  2103.6 4.4 add_convert_fusion.1
  2108.1 3.9 fusion.196
  2112.1 4.4 add_convert_fusion.2
  2130.8 4.4 collective-permute-done.15
  2159.3 87.9 %all-reduce.6 = (f32[1024]{0:T(1024)S(1)}, f32[1024]{0:T(1024)S(1)}) all-reduce(f32[1024]{0:T(1024)S(1)} %add.424, f32[1024]{0:T(1024)S(1)} %copy-done.163), channel_id=2, replica_groups=mesh['dp'=16,'expert'=8] {'dp','expert'}, use_global_device_ids=true, to_apply=%region_56.59.clone | all-reduce | flops 2048 | bytes 16384
  2249.5 6.3 all-reduce.11.cloned.1.call-done
  2258.4 67.4 %reduce-scatter.20.cloned.1.call-done = bf16[4,32,1024]{2,1,0:T(8,128)(2,1)} async-done(((bf16[4,512,1024]{2,1,0:T(8,128)(2,1)}), bf16[4,32,1024]{2,1,0:T(8,128)(2,1)}) %reduce-scatter.20.cloned.1.call-update) | async-done | bytes 262160 | tf_op jit(solution)/shard_map/reduce_scatter | solution.py:473
  2327.6 68.9 %reduce-scatter.18.cloned.1.call-done = bf16[4,64,512]{2,1,0:T(8,128)(2,1)} async-done(((bf16[4,1024,512]{2,1,0:T(8,128)(2,1)}), bf16[4,64,512]{2,1,0:T(8,128)(2,1)}) %reduce-scatter.18.cloned.1.call-update) | async-done | bytes 262160 | tf_op jit(solution)/shard_map/reduce_scatter | solution.py:470
  2398.2 69.1 %reduce-scatter.16.cloned.1.call-done = bf16[4,64,512]{2,1,0:T(8,128)(2,1)} async-done(((bf16[4,1024,512]{2,1,0:T(8,128)(2,1)}), bf16[4,64,512]{2,1,0:T(8,128)(2,1)}) %reduce-scatter.16.cloned.1.call-update) | async-done | bytes 262160 | tf_op jit(solution)/shard_map/reduce_scatter | solution.py:467
  2469.2 640.1 %reduce-scatter.12.cloned.1.call-done = f32[8,512]{1,0:T(8,128)} async-done(((f32[1024,512]{1,0:T(8,128)}), f32[8,512]{1,0:T(8,128)}) %reduce-scatter.12.cloned.1.call-update) | async-done | bytes 16400 | tf_op jit(solution)/shard_map/reduce_scatter | solution.py:460
  3109.3 638.6 %reduce-scatter.10.cloned.1.call-done = f32[8,512]{1,0:T(8,128)} async-done(((f32[1024,512]{1,0:T(8,128)}), f32[8,512]{1,0:T(8,128)}) %reduce-scatter.10.cloned.1.call-update) | async-done | bytes 16400 | tf_op jit(solution)/shard_map/reduce_scatter | solution.py:459
  3747.9 642.1 %reduce-scatter.14.cloned.1.call-done = f32[8,1024]{1,0:T(8,128)} async-done(((f32[1024,1024]{1,0:T(8,128)}), f32[8,1024]{1,0:T(8,128)}) %reduce-scatter.14.cloned.1.call-update) | async-done | bytes 32784 | tf_op jit(solution)/shard_map/reduce_scatter | solution.py:461
  4390.0 641.7 %reduce-scatter.8.cloned.1.call-done = f32[8,1024]{1,0:T(8,128)} async-done(((f32[1024,1024]{1,0:T(8,128)}), f32[8,1024]{1,0:T(8,128)}) %reduce-scatter.8.cloned.1.call-update) | async-done | bytes 32784 | tf_op jit(solution)/shard_map/reduce_scatter | solution.py:458
  (663 shorter events, 201.3 us)
Async XLA Ops:
  7.2 296.8 %copy-start.17 = (bf16[2,1,128,1024]{3,2,1,0:T(8,128)(2,1)S(1)}, bf16[2,1,128,1024]{3,2,1,0:T(8,128)(2,1)}, u32[]{:S(2)}) copy-start(bf16[2,1,128,1024]{3,2,1,0:T(8,128)(2,1)} %param.21) | copy-start | bytes 1572868
  7.2 296.8 %all-gather.8.cloned.1.call-start = ((), (), s32[]{:S(2)}) async-start(), calls=%async_computation.15 | async-start | bytes 1056768 | tf_op jit(solution)/shard_map/all_gather | solution.py:118
  7.9 590.7 %all-gather.10.cloned.1.call-start = ((), (), s32[]{:S(2)}) async-start(), calls=%async_computation.16 | async-start | bytes 1056768 | tf_op jit(solution)/shard_map/all_gather | solution.py:117
  8.7 889.8 %all-gather.12.cloned.1.call-start = ((), (), s32[]{:S(2)}) async-start(), calls=%async_computation.17 | async-start | bytes 2113536 | tf_op jit(solution)/shard_map/all_gather | solution.py:116
  9.4 1191.4 %all-gather.14.cloned.1.call-start = ((), (), s32[]{:S(2)}) async-start(), calls=%async_computation.18 | async-start | bytes 2113536 | tf_op jit(solution)/shard_map/all_gather | solution.py:119
  10.0 1267.3 %all-gather.16.cloned.1.call-start = ((), (), s32[]{:S(2)}) async-start(), calls=%async_computation.19 | async-start | bytes 4456448 | tf_op jit(solution)/shard_map/all_gather | solution.py:124
  10.6 1283.7 %all-gather.18.cloned.1.call-start = ((), (), s32[]{:S(2)}) async-start(), calls=%async_computation.20 | async-start | bytes 4456448 | tf_op jit(solution)/shard_map/all_gather | solution.py:125
  11.1 1322.8 %all-gather.20.cloned.1.call-start = ((), (), s32[]{:S(2)}) async-start(), calls=%async_computation.21 | async-start | bytes 4456448 | tf_op jit(solution)/shard_map/all_gather | solution.py:126
  15.4 587.1 %copy-start.170 = (f32[64]{0:T(128)}, f32[64]{0:T(128)S(1)}, u32[]{:S(2)}) copy-start(f32[64]{0:T(128)S(1)} %convert_element_type.453) | copy-start | bytes 772
  87.6 1687.5 %copy-start.111 = (f32[1024]{0:T(1024)}, f32[1024]{0:T(1024)S(1)}, u32[]{:S(2)}) copy-start(f32[1024]{0:T(1024)S(1)} %convert_element_type.445) | copy-start | bytes 12292
  87.9 817.4 %copy-start.95 = (f32[128,64]{0,1:T(8,128)}, f32[128,64]{0,1:T(8,128)S(1)}, u32[]{:S(2)}) copy-start(f32[128,64]{0,1:T(8,128)S(1)} %get-tuple-element.164) | copy-start | bytes 98308
  87.9 817.4 %copy-start.97 = (f32[128,64]{0,1:T(8,128)}, f32[128,64]{0,1:T(8,128)S(1)}, u32[]{:S(2)}) copy-start(f32[128,64]{0,1:T(8,128)S(1)} %get-tuple-element.165) | copy-start | bytes 98308
  98.2 503.1 %copy-start.153 = (f32[128]{0:T(128)}, f32[128]{0:T(128)S(1)}, u32[]{:S(2)}) copy-start(f32[128]{0:T(128)S(1)} %get-tuple-element.240) | copy-start | bytes 1540
  98.2 803.2 %copy-start.149 = (f32[128]{0:T(128)}, f32[128]{0:T(128)S(1)}, u32[]{:S(2)}) copy-start(f32[128]{0:T(128)S(1)} %get-tuple-element.192) | copy-start | bytes 1540
  99.7 806.6 %copy-start.101 = (pred[128,384]{0,1:T(8,128)(4,1)}, pred[128,384]{0,1:T(8,128)(4,1)S(1)}, u32[]{:S(2)}) copy-start(pred[128,384]{0,1:T(8,128)(4,1)S(1)} %get-tuple-element.181) | copy-start | bytes 147460
  305.6 306.1 %collective-permute-start.1 = (bf16[128,512]{1,0:T(8,128)(2,1)S(1)}, bf16[128,512]{1,0:T(8,128)(2,1)S(1)}, u32[]{:S(2)}, u32[]{:S(2)}) collective-permute-start(bf16[128,512]{1,0:T(8,128)(2,1)S(1)} %convolution_convert_fusion.3), channel_id=1, source_target_pairs={{0,1},{1,2},{2,3},{3,4},{4,5},{5,6},{6,7},{8,9},{9,10},{10,11},{11... | collective-permute-start | bytes 393224 | tf_op jit(solution)/shard_map/ppermute | solution.py:18
  310.5 301.2 %collective-permute-start = (bf16[128,512]{1,0:T(8,128)(2,1)S(1)}, bf16[128,512]{1,0:T(8,128)(2,1)S(1)}, u32[]{:S(2)}, u32[]{:S(2)}) collective-permute-start(bf16[128,512]{1,0:T(8,128)(2,1)S(1)} %convolution_convert_fusion.3), channel_id=1, source_target_pairs={{0,2},{1,3},{2,4},{3,5},{4,6},{5,7},{8,10},{9,11},{10,12},{11,13},... | collective-permute-start | bytes 393224 | tf_op jit(solution)/shard_map/ppermute | solution.py:18
  603.8 302.5 %copy-start.107 = (bf16[128,8,64]{0,2,1:T(8,128)(2,1)}, bf16[128,8,64]{0,2,1:T(8,128)(2,1)S(1)}, u32[]{:S(2)}) copy-start(bf16[128,8,64]{0,2,1:T(8,128)(2,1)S(1)} %get-tuple-element.150) | copy-start | bytes 393220
  603.8 302.4 %collective-permute-start.3 = (bf16[128,512]{0,1:T(8,128)(2,1)S(1)}, bf16[128,512]{0,1:T(8,128)(2,1)S(1)}, u32[]{:S(2)}, u32[]{:S(2)}) collective-permute-start(bf16[128,512]{0,1:T(8,128)(2,1)S(1)} %bitcast.584), channel_id=1, source_target_pairs={{0,1},{1,2},{2,3},{3,4},{4,5},{5,6},{6,7},{8,9},{9,10},{10,11},{11... | collective-permute-start | bytes 393224 | tf_op jit(solution)/shard_map/ppermute | solution.py:18
  608.8 297.4 %collective-permute-start.2 = (bf16[128,512]{0,1:T(8,128)(2,1)S(1)}, bf16[128,512]{0,1:T(8,128)(2,1)S(1)}, u32[]{:S(2)}, u32[]{:S(2)}) collective-permute-start(bf16[128,512]{0,1:T(8,128)(2,1)S(1)} %bitcast.585), channel_id=1, source_target_pairs={{0,2},{1,3},{2,4},{3,5},{4,6},{5,7},{8,10},{9,11},{10,12},{11,13},... | collective-permute-start | bytes 393224 | tf_op jit(solution)/shard_map/ppermute | solution.py:18
  612.0 295.5 %copy-start.76 = (bf16[384,512]{0,1:T(8,128)(2,1)}, bf16[384,512]{0,1:T(8,128)(2,1)S(1)}, u32[]{:S(2)}) copy-start(bf16[384,512]{0,1:T(8,128)(2,1)S(1)} %copy.157) | copy-start | bytes 1179652
  909.5 294.2 %copy-start.87 = (bf16[8,64,2,128]{3,1,2,0:T(8,128)(2,1)}, bf16[8,64,2,128]{3,1,2,0:T(8,128)(2,1)S(1)}, u32[]{:S(2)}) copy-start(bf16[8,64,2,128]{3,1,2,0:T(8,128)(2,1)S(1)} %fusion.57) | copy-start | bytes 786436
  1203.5 73.3 %copy-start.182 = (f32[128]{0:T(128)}, f32[128]{0:T(128)S(1)}, u32[]{:S(2)}) copy-start(f32[128]{0:T(128)S(1)} %get-tuple-element.198) | copy-start | bytes 1540
  1203.7 73.1 %copy-start.55 = (bf16[128,1024]{1,0:T(8,128)(2,1)}, bf16[128,1024]{1,0:T(8,128)(2,1)S(1)}, u32[]{:S(2)}) copy-start(bf16[128,1024]{1,0:T(8,128)(2,1)S(1)} %multiply_convert_fusion.7) | copy-start | bytes 786436
  1277.2 17.0 copy-start.11
  1342.6 349.0 %copy-start.189 = (s32[2,1,128]{2,1,0:T(1,128)S(1)}, s32[2,1,128]{2,1,0:T(1,128)}, u32[]{:S(2)}) copy-start(s32[2,1,128]{2,1,0:T(1,128)} %param.25) | copy-start | bytes 3076
  1342.6 352.8 %copy-start.139 = (s32[128,8]{0,1:T(8,128)S(1)}, s32[128,8]{0,1:T(8,128)}, u32[]{:S(2)}) copy-start(s32[128,8]{0,1:T(8,128)} %get-tuple-element.170) | copy-start | bytes 12292
  1342.6 352.9 %all-to-all-start.1 = ((bf16[1,4,384,1024]{3,1,0,2:T(4,128)(2,1)}), bf16[1,4,384,1024]{3,1,0,2:T(4,128)(2,1)S(1)}, u32[]{:S(2)}, u32[]{:S(2)}) async-start(bf16[1,4,384,1024]{3,1,0,2:T(4,128)(2,1)} %copy.168), calls=%async_computation.1 | async-start | bytes 6291456 | tf_op jit(solution)/shard_map/all_to_all | solution.py:234
  1691.6 14.0 copy-start.166
  1717.1 34.6 all-to-all-start.4
  1770.0 14.2 copy-start.109
  1770.0 44.1 all-to-all-start.5
  1774.6 34.9 copy-start.93
  1774.6 34.9 copy-start.99
  1775.5 27.3 collective-permute-start.5
  1780.8 27.3 collective-permute-start.4
  1784.2 24.2 collective-permute-start.7
  1787.6 21.9 collective-permute-start.6
  1813.5 20.9 copy-start.49
  1814.0 20.4 copy-start.180
  1897.0 33.8 all-to-all-start.3
  1901.2 39.5 copy-start.168
  1950.7 34.5 copy-start.194
  1999.9 34.8 all-to-all-start.7
  2004.4 251.4 %all-reduce.11.cloned.1.call-start = ((), (), s32[]{:S(2)}) async-start(), calls=%async_computation.29 | async-start | bytes 1179648
  2073.3 8.8 collective-permute-start.13
  2074.7 8.4 collective-permute-start.12
  2076.1 8.1 collective-permute-start.9
  2077.4 9.0 collective-permute-start.8
  2088.9 236.8 %reduce-scatter.20.cloned.1.call-start = ((), (), s32[]{:S(2)}) async-start(), calls=%async_computation.28 | async-start | bytes 4456448 | tf_op jit(solution)/shard_map/reduce_scatter | solution.py:473
  2097.8 298.7 %reduce-scatter.18.cloned.1.call-start = ((), (), s32[]{:S(2)}) async-start(), calls=%async_computation.27 | async-start | bytes 4456448 | tf_op jit(solution)/shard_map/reduce_scatter | solution.py:470
  2108.0 359.3 %reduce-scatter.16.cloned.1.call-start = ((), (), s32[]{:S(2)}) async-start(), calls=%async_computation.26 | async-start | bytes 4456448 | tf_op jit(solution)/shard_map/reduce_scatter | solution.py:467
  2116.5 992.8 %reduce-scatter.12.cloned.1.call-start = ((), (), s32[]{:S(2)}) async-start(), calls=%async_computation.24 | async-start | bytes 2113536 | tf_op jit(solution)/shard_map/reduce_scatter | solution.py:460
  2120.2 8.2 collective-permute-start.11
  2121.5 9.2 collective-permute-start.10
  2123.0 12.2 copy-start.19
  2123.8 11.4 collective-permute-start.15
  2125.1 10.1 collective-permute-start.14
  2137.9 1610.1 %reduce-scatter.10.cloned.1.call-start = ((), (), s32[]{:S(2)}) async-start(), calls=%async_computation.23 | async-start | bytes 2113536 | tf_op jit(solution)/shard_map/reduce_scatter | solution.py:459
  2140.8 2249.2 %reduce-scatter.14.cloned.1.call-start = ((), (), s32[]{:S(2)}) async-start(), calls=%async_computation.25 | async-start | bytes 4227072 | tf_op jit(solution)/shard_map/reduce_scatter | solution.py:461
  2144.7 2887.1 %reduce-scatter.8.cloned.1.call-start = ((), (), s32[]{:S(2)}) async-start(), calls=%async_computation.22 | async-start | bytes 4227072 | tf_op jit(solution)/shard_map/reduce_scatter | solution.py:458
  2158.0 90.4 %copy-start.45 = (f32[128,1024]{1,0:T(8,128)S(1)}, f32[128,1024]{1,0:T(8,128)}, u32[]{:S(2)}) copy-start(f32[128,1024]{1,0:T(8,128)} %copy-done.43) | copy-start | bytes 1572868
  2158.0 90.3 %copy-start.186 = (f32[128]{0:T(128)S(1)}, f32[128]{0:T(128)}, u32[]{:S(2)}) copy-start(f32[128]{0:T(128)} %get-tuple-element.191) | copy-start | bytes 1540
  2158.0 90.3 %copy-start.187 = (f32[128]{0:T(128)S(1)}, f32[128]{0:T(128)}, u32[]{:S(2)}) copy-start(f32[128]{0:T(128)} %get-tuple-element.241) | copy-start | bytes 1540
  (169 other events, 600.8 us)
Sparse Core Ops, SparseCore 0:
  9.7 294.2 all-gather.7
  305.7 292.9 all-gather.9
  600.4 298.0 all-gather.11
  900.0 300.7 all-gather.13
  1202.3 51.6 all-gather.15
  1255.6 38.6 all-gather.17
  1295.9 38.0 all-gather.19
  2089.0 166.7 all-reduce.10
  2258.4 67.3 reduce-scatter.19
  2328.2 68.2 reduce-scatter.17
  2399.0 68.3 reduce-scatter.15
  2470.2 638.9 reduce-scatter.11
  3112.2 635.6 reduce-scatter.9
  3750.8 639.1 reduce-scatter.13
  4392.8 638.9 reduce-scatter.7
where the time goes:
time: 5050 us; the launch traced here: 5040 us
  waiting for transfers between devices  3980 us (79%)
  blocking collectives  637 us (13%)
  local copies, waits for them, and re-layouts  128 us (3%)
  matrix products  121 us (2%)
  other arithmetic  91.8 us (2%)
  starting transfers between devices  67.5 us (1%)
    reduce_scatter x1, waiting for transfers between devices, body(): lax.psum_scatter(acc_out, ('dp', 'expert'), scatter_dimension=0, tiled=True)  642 us
    reduce_scatter x1, waiting for transfers between devices, body(): lax.psum_scatter(acc_query, ('dp', 'expert'), scatter_dimension=0, tiled=...  642 us
    reduce_scatter x1, waiting for transfers between devices, body(): lax.psum_scatter(acc_value, ('dp', 'expert'), scatter_dimension=0, tiled=...  640 us
    reduce_scatter x1, waiting for transfers between devices, body(): lax.psum_scatter(acc_key, ('dp', 'expert'), scatter_dimension=0, tiled=True)  639 us
    all_gather x1, blocking collectives, fetch_all(): lax.all_gather(w_router, ('dp', 'expert'), axis=0, tiled=True)  342 us
    all_gather x1, waiting for transfers between devices, fetch_all(): lax.all_gather(w_out, ('dp', 'expert'), axis=0, tiled=True)  291 us
    all_gather x1, waiting for transfers between devices, fetch_all(): lax.all_gather(w_query, ('dp', 'expert'), axis=0, tiled=True)  286 us
    all_gather x1, waiting for transfers between devices, fetch_all(): lax.all_gather(w_key, ('dp', 'expert'), axis=0, tiled=True)  285 us
  transfers between devices with their start and end apart: 36, of which 26 were waited for; matrix products, arithmetic and copies ran while one was open for 3% of the time, Pallas kernels for 0%

commit v1 on v0

v1 whole, which is shorter than its diff:
```python
import math

import jax
import jax.numpy as jnp
from jax import lax
from jax.sharding import PartitionSpec as P

WINDOW = 256
EPSILON = 1e-06
ROPE_BASE = 10000.0
CAP = 48

bf16 = jnp.bfloat16
f32 = jnp.float32


def rms_scale(values):
    return lax.rsqrt(jnp.mean(values * values, axis=-1, keepdims=True) + EPSILON)


def rope_tables(positions, head_size):
    half_size = head_size // 2
    frequency = jnp.exp(
        -math.log(ROPE_BASE) * (2.0 * jnp.arange(half_size, dtype=f32) / head_size)
    )
    angles = positions.astype(f32)[:, None] * frequency[None, :]
    angles = jnp.concatenate([angles, angles], axis=-1)
    return (jnp.cos(angles), jnp.sin(angles))


def rotate(values, cosine, sine):
    half_size = values.shape[-1] // 2
    turned = jnp.concatenate([-values[..., half_size:], values[..., :half_size]], axis=-1)
    return values * cosine[:, None, :] + turned * sine[:, None, :]


def rotate_back(upstream, cosine, sine):
    half_size = upstream.shape[-1] // 2
    scaled = upstream * sine[:, None, :]
    turned = jnp.concatenate([scaled[..., half_size:], -scaled[..., :half_size]], axis=-1)
    return upstream * cosine[:, None, :] + turned


def norm_back(upstream, values, scaling):
    return scaling * upstream - values * (scaling * scaling * scaling) * jnp.mean(
        upstream * values, axis=-1, keepdims=True
    )


def product(left_side, right_side):
    return jnp.dot(left_side, right_side, preferred_element_type=f32)


def product_tn(left_side, right_side):
    return lax.dot_general(
        left_side, right_side, (((0,), (0,)), ((), ())), preferred_element_type=f32
    )


def product_nt(left_side, right_side):
    return lax.dot_general(
        left_side, right_side, (((1,), (1,)), ((), ())), preferred_element_type=f32
    )


def einsum(spec, left_side, right_side):
    return jnp.einsum(spec, left_side, right_side, preferred_element_type=f32)


def spread(values, axis):
    count = lax.axis_size(axis)
    return lax.all_to_all(jnp.broadcast_to(values[None], (count,) + values.shape), axis, 0, 0)


def passed_along(value, axis, steps):
    count = lax.axis_size(axis)
    initial, last = (max(0, -steps), min(count, count - steps))
    return lax.ppermute(value, axis, [(source, source + steps) for source in range(initial, last)])


def sum_to_owner(parts):
    count = lax.axis_size("dp")
    half = count // 2
    core = lax.axis_index("dp") % 2
    pairs = parts.reshape((half, 2) + parts.shape[1:])
    kept = lax.dynamic_index_in_dim(pairs, core, 1, keepdims=False)
    sent = lax.dynamic_index_in_dim(pairs, 1 - core, 1, keepdims=False)
    received = lax.ppermute(sent, "dp", [(i, i ^ 1) for i in range(count)])
    both = (kept.astype(f32) + received.astype(f32)).astype(bf16)
    groups = [[2 * i + c for i in range(half)] for c in range(2)]
    arrived = lax.all_to_all(both, "dp", 0, 0, axis_index_groups=groups)
    return jnp.sum(arrived.astype(f32), axis=0)


def body(
    tokens,
    cotangent,
    routes,
    doc_lengths,
    valid,
    attn_gain,
    w_query,
    w_key,
    w_value,
    query_gain,
    key_gain,
    w_out,
    ffn_gain,
    w_router,
    w_gate,
    w_up,
    w_down,
):
    micro = tokens.shape[0]
    rows = tokens.shape[2]
    width = tokens.shape[3]
    head_size = query_gain.shape[0]
    q_width = w_query.shape[1]
    kv_width = w_key.shape[1]
    kv_heads = kv_width // head_size
    q_heads = q_width // head_size
    group_size = q_heads // kv_heads
    experts = w_router.shape[1]
    local = w_gate.shape[0]
    hidden_width = w_gate.shape[2]
    expert_devices = lax.axis_size("expert")
    dp_devices = lax.axis_size("dp")
    own_rows = w_query.shape[0]
    reach_back = (WINDOW + rows - 2) // rows
    key_rows = rows * (reach_back + 1)
    score_scale = 1.0 / math.sqrt(head_size)
    q_gain = query_gain.astype(f32)
    k_gain = key_gain.astype(f32)
    all_rows = micro * rows
    qkv_width = q_width + 2 * kv_width

    gains = jnp.concatenate([attn_gain[:, None], ffn_gain[:, None]], axis=1)
    tail = jnp.concatenate(
        [w_router, gains, jnp.zeros((own_rows, 128 - experts - 2), bf16)], axis=1
    )
    packed = jnp.concatenate([w_query, w_key, w_value, w_out, tail], axis=1)
    packed = spread(packed, "expert").reshape(expert_devices * own_rows, packed.shape[1])
    dense = lax.all_gather(packed, "dp", axis=0, tiled=True)
    qkv_full = dense[:, :qkv_width]
    out_full = dense[:, qkv_width : qkv_width + width]
    router_full = dense[:, qkv_width + width : qkv_width + width + experts]
    gain_attn = dense[:, qkv_width + width + experts].astype(f32)
    gain_ffn = dense[:, qkv_width + width + experts + 1].astype(f32)
    gate_up_full = lax.all_gather(
        jnp.concatenate([w_gate, w_up], axis=2), "dp", axis=1, tiled=True
    )
    down_full = lax.all_gather(w_down, "dp", axis=1, tiled=True)

    seed_low = cotangent[:, 0] * valid[:, 0][:, :, None].astype(bf16)
    out_seed = seed_low.astype(f32).reshape(all_rows, width)
    seed_all = spread(seed_low, "expert").reshape(expert_devices * micro, rows, width)
    routes_all = spread(routes[:, 0], "expert").reshape(expert_devices * micro, rows, -1)
    expert_ids = jnp.arange(experts, dtype=jnp.int32)
    member_all = jnp.any(routes_all[..., None] == expert_ids, axis=2)
    expert_index = lax.axis_index("expert")
    member = lax.dynamic_slice_in_dim(member_all, expert_index * local, local, 2)
    earlier = (
        jnp.arange(rows, dtype=jnp.int32)[:, None] > jnp.arange(rows, dtype=jnp.int32)[None, :]
    ).astype(bf16)
    rank = einsum("ut,btj->bju", earlier, member.astype(bf16)).astype(jnp.int32)
    slots = jnp.where(member.transpose(0, 2, 1), rank, -1)
    picks = slots[:, :, None, :] == jnp.arange(CAP, dtype=jnp.int32)[:, None]
    pick_low = picks.astype(bf16)

    q_pos = expert_index * rows + jnp.arange(rows, dtype=jnp.int32)
    k_pos = (expert_index - reach_back) * rows + jnp.arange(key_rows, dtype=jnp.int32)
    cosine, sine = rope_tables(q_pos, head_size)
    cosine = jnp.concatenate([cosine] * micro, axis=0)
    sine = jnp.concatenate([sine] * micro, axis=0)
    bounds = jnp.cumsum(doc_lengths[:, 0], axis=1)
    q_doc = jnp.sum((q_pos[None, :, None] >= bounds[:, None, :]).astype(jnp.int32), axis=2)
    k_doc = jnp.sum((k_pos[None, :, None] >= bounds[:, None, :]).astype(jnp.int32), axis=2)
    offset = q_pos[:, None] - k_pos[None, :]
    visible = (
        (k_pos[None, None, :] >= 0)
        & (q_doc[:, :, None] == k_doc[:, None, :])
        & (offset >= 0)[None]
        & (offset < WINDOW)[None]
    )[:, None, None]

    x_float = tokens[:, 0].reshape(all_rows, width).astype(f32)
    attn_scale = rms_scale(x_float)
    normed = (x_float * attn_scale * gain_attn).astype(bf16)
    qkv = product(normed, qkv_full)
    query = qkv[:, :q_width].reshape(all_rows, q_heads, head_size)
    key_pre = qkv[:, q_width : q_width + kv_width].reshape(all_rows, kv_heads, head_size)
    value_low = qkv[:, q_width + kv_width :].astype(bf16)
    query_scale = rms_scale(query)
    key_scale = rms_scale(key_pre)
    query_rot = rotate(query * query_scale * q_gain, cosine, sine).astype(bf16)
    key_rot = rotate(key_pre * key_scale * k_gain, cosine, sine).astype(bf16)
    key_value = jnp.concatenate([key_rot.reshape(all_rows, kv_width), value_low], axis=1)
    key_value = key_value.reshape(micro, rows, 2 * kv_width)
    parts = [key_value]
    for distance in range(1, reach_back + 1):
        parts = [passed_along(key_value, "expert", distance)] + parts
    key_value = jnp.concatenate(parts, axis=1)
    keys_all = key_value[..., :kv_width].reshape(micro, key_rows, kv_heads, head_size)
    values_all = key_value[..., kv_width:].reshape(micro, key_rows, kv_heads, head_size)
    query_group = query_rot.reshape(micro, rows, kv_heads, group_size, head_size)
    scores = einsum("mtkgd,mskd->mkgts", query_group, keys_all) * score_scale
    scores = jnp.where(visible, scores, -1e30)
    row_peak = jnp.max(scores, axis=-1, keepdims=True)
    exp_scores = jnp.exp(scores - row_peak)
    attn_probs = exp_scores / jnp.sum(exp_scores, axis=-1, keepdims=True)
    probs_low = attn_probs.astype(bf16)
    attended = einsum("mkgts,mskd->mtkgd", probs_low, values_all)
    attended = attended.reshape(all_rows, q_width).astype(bf16)
    middle = x_float + product(attended, out_full)
    ffn_scale = rms_scale(middle)
    moe_in = (middle * ffn_scale * gain_ffn).astype(bf16)

    moe_all = spread(moe_in.reshape(micro, rows, width), "expert")
    moe_all = moe_all.reshape(expert_devices * micro, rows, width)
    logits_all = einsum("btd,de->bte", moe_all, router_full)
    gates_all = jax.nn.softmax(jnp.where(member_all, logits_all, -1e30), axis=-1)
    gates_all = jnp.where(member_all, gates_all, 0.0)
    gates = lax.dynamic_slice_in_dim(gates_all, expert_index * local, local, 2)
    row_gates = jnp.sum(
        jnp.where(picks, gates.transpose(0, 2, 1)[:, :, None, :], 0.0), axis=-1
    ).transpose(1, 0, 2).reshape(local, -1)
    slot_rows = expert_devices * micro * CAP
    arrived = einsum("bjct,btd->jbcd", pick_low, moe_all).astype(bf16)
    arrived = arrived.reshape(local, slot_rows, width)
    seed_rows = einsum("bjct,btd->jbcd", pick_low, seed_all)
    seed_rows = seed_rows.reshape(local, slot_rows, width)
    out_rows = (row_gates[:, :, None] * seed_rows).astype(bf16)
    pre = einsum("ecd,edf->ecf", arrived, gate_up_full)
    gate_pre = pre[..., :hidden_width]
    up_pre = pre[..., hidden_width:]
    sigma = jax.nn.sigmoid(gate_pre)
    gate_act = gate_pre * sigma
    hidden = (gate_act * up_pre).astype(bf16)
    expert_out = einsum("ecf,efd->ecd", hidden, down_full).astype(bf16).astype(f32)
    row_grads = jnp.sum(expert_out * seed_rows, axis=-1)
    mixed_rows = (row_gates[:, :, None] * expert_out).astype(bf16)
    hidden_grad = einsum("ecd,efd->ecf", out_rows, down_full)
    down_grad = einsum("ecf,ecd->efd", hidden, out_rows).astype(bf16)
    gate_low = (hidden_grad * up_pre * sigma * (1.0 + gate_pre * (1.0 - sigma))).astype(bf16)
    up_low = (hidden_grad * gate_act).astype(bf16)
    pre_low = jnp.concatenate([gate_low, up_low], axis=2)
    gate_up_grad = einsum("ecd,ecf->edf", arrived, pre_low).astype(bf16)
    row_back = einsum("ecf,edf->ecd", pre_low, gate_up_full).astype(bf16)

    blocks = (local, expert_devices * micro, CAP)
    back_part = einsum("bjct,jbcd->btd", pick_low, row_back.reshape(blocks + (width,)))
    back_part = back_part.astype(bf16).reshape(expert_devices, micro, rows, width)
    out_part = einsum("bjct,jbcd->btd", pick_low, mixed_rows.reshape(blocks + (width,)))
    out_part = out_part.astype(bf16).reshape(expert_devices, micro, rows, width)
    row_grads = row_grads.reshape(blocks).transpose(1, 0, 2)
    gate_part = jnp.sum(jnp.where(picks, row_grads[..., None], 0.0), axis=2)
    gate_part = gate_part.reshape(expert_devices, micro, local, rows)
    gate_back = lax.all_to_all(gate_part, "expert", 0, 0)
    moe_back = lax.all_to_all(back_part, "expert", 0, 0)
    out_back = lax.all_to_all(out_part, "expert", 0, 0)

    own_gate_up = sum_to_owner(
        gate_up_grad.reshape(local, dp_devices, -1, 2 * hidden_width).transpose(1, 0, 2, 3)
    )
    own_down = sum_to_owner(down_grad.reshape(local, dp_devices, -1, width).transpose(1, 0, 2, 3))

    gate_grad = gate_back.transpose(1, 3, 0, 2).reshape(all_rows, experts)
    own_member = lax.dynamic_slice_in_dim(member_all, expert_index * micro, micro, 0)
    own_logits = product(moe_in, router_full)
    own_member = own_member.reshape(all_rows, experts)
    own_gates = jax.nn.softmax(jnp.where(own_member, own_logits, -1e30), axis=-1)
    own_gates = jnp.where(own_member, own_gates, 0.0)
    logit_grad = own_gates * (
        gate_grad - jnp.sum(own_gates * gate_grad, axis=-1, keepdims=True)
    )
    logit_grad = logit_grad.astype(bf16)
    router_grad = product_tn(moe_in, logit_grad)
    moe_grad = product_nt(logit_grad, router_full) + jnp.sum(
        moe_back.astype(f32), axis=0
    ).reshape(all_rows, width)
    ffn_gain_grad = jnp.sum(moe_grad * middle * ffn_scale, axis=0)
    mid_grad = out_seed + norm_back(moe_grad * gain_ffn, middle, ffn_scale)
    branch_low = mid_grad.astype(bf16)
    out_grad = product_tn(attended, branch_low)
    attended_grad = product_nt(branch_low, out_full).astype(bf16)
    attended_grad = attended_grad.reshape(micro, rows, kv_heads, group_size, head_size)
    first_sum = sum_to_owner(
        jnp.concatenate(
            [
                out_grad.astype(bf16),
                jnp.concatenate(
                    [router_grad, ffn_gain_grad[:, None], jnp.zeros((width, 128 - experts - 1), f32)],
                    axis=1,
                ).astype(bf16),
            ],
            axis=1,
        ).reshape(dp_devices, expert_devices * own_rows, width + 128)
    )

    prob_grad = einsum("mtkgd,mskd->mkgts", attended_grad, values_all)
    inner = jnp.sum(attn_probs * prob_grad, axis=-1, keepdims=True)
    score_low = (score_scale * attn_probs * (prob_grad - inner)).astype(bf16)
    value_grad = einsum("mkgts,mtkgd->mskd", probs_low, attended_grad)
    query_rot_grad = einsum("mkgts,mskd->mtkgd", score_low, keys_all)
    key_rot_grad = einsum("mkgts,mtkgd->mskd", score_low, query_group)
    both_grad = jnp.concatenate(
        [
            key_rot_grad.reshape(micro, key_rows, kv_width),
            value_grad.reshape(micro, key_rows, kv_width),
        ],
        axis=2,
    )
    start_local = reach_back * rows
    local_grad = both_grad[:, start_local:]
    for distance in range(1, reach_back + 1):
        first_row = (reach_back - distance) * rows
        local_grad = local_grad + passed_along(
            both_grad[:, first_row : first_row + rows].astype(bf16), "expert", -distance
        ).astype(f32)
    local_grad = local_grad.reshape(all_rows, 2 * kv_width)
    value_low_grad = local_grad[:, kv_width:].astype(bf16)
    key_norm_grad = rotate_back(
        local_grad[:, :kv_width].reshape(all_rows, kv_heads, head_size), cosine, sine
    )
    key_gain_grad = jnp.sum(key_norm_grad * key_pre * key_scale, axis=(0, 1))
    key_low = norm_back(key_norm_grad * k_gain, key_pre, key_scale).astype(bf16)
    query_norm_grad = rotate_back(
        query_rot_grad.reshape(all_rows, q_heads, head_size), cosine, sine
    )
    query_gain_grad = jnp.sum(query_norm_grad * query * query_scale, axis=(0, 1))
    query_low = norm_back(query_norm_grad * q_gain, query, query_scale).astype(bf16)
    qkv_low = jnp.concatenate(
        [query_low.reshape(all_rows, q_width), key_low.reshape(all_rows, kv_width), value_low_grad],
        axis=1,
    )
    qkv_grad = product_tn(normed, qkv_low)
    normed_grad = product_nt(qkv_low, qkv_full)
    attn_gain_grad = jnp.sum(normed_grad * x_float * attn_scale, axis=0)
    token_grad = mid_grad + norm_back(normed_grad * gain_attn, x_float, attn_scale)

    head_gains = jnp.concatenate([query_gain_grad, key_gain_grad])
    owners = width // own_rows
    extra = jnp.concatenate(
        [
            jnp.broadcast_to(head_gains[None, None], (owners, 1, 2 * head_size)),
            jnp.pad(
                attn_gain_grad.reshape(owners, 1, own_rows),
                ((0, 0), (0, own_rows - 2), (0, 2 * head_size - own_rows)),
            ),
        ],
        axis=1,
    ).reshape(width, 2 * head_size)
    last_sum = sum_to_owner(
        jnp.concatenate([qkv_grad.astype(bf16), extra.astype(bf16)], axis=1).reshape(
            dp_devices, expert_devices * own_rows, qkv_width + 2 * head_size
        )
    )
    dense_sum = jnp.concatenate([first_sum, last_sum], axis=1).astype(bf16)
    dense_sum = dense_sum.reshape(expert_devices, own_rows, -1)
    owned = jnp.sum(lax.all_to_all(dense_sum, "expert", 0, 0).astype(f32), axis=0)
    out_owned = owned[:, :width]
    router_owned = owned[:, width : width + experts]
    ffn_gain_owned = owned[:, width + experts]
    base = width + 128
    extra_owned = owned[:, base + qkv_width :]

    output = middle + jnp.sum(out_back.astype(f32), axis=0).reshape(all_rows, width)
    return (
        output.astype(bf16).reshape(micro, 1, rows, width),
        token_grad.astype(bf16).reshape(micro, 1, rows, width),
        extra_owned[1, :own_rows],
        owned[:, base : base + q_width],
        owned[:, base + q_width : base + q_width + kv_width],
        owned[:, base + q_width + kv_width : base + qkv_width],
        extra_owned[0, :head_size],
        extra_owned[0, head_size:],
        out_owned,
        ffn_gain_owned,
        router_owned,
        own_gate_up[..., :hidden_width],
        own_gate_up[..., hidden_width:],
        own_down,
    )


def solution(mesh):
    rows_spec = P(("dp", "expert"), None)
    gain_spec = P(("dp", "expert"))
    token_spec = P(None, "dp", "expert", None)
    expert_spec = P("expert", "dp", None)
    return jax.shard_map(
        body,
        mesh=mesh,
        in_specs=(
            token_spec,
            token_spec,
            token_spec,
            P(None, "dp", None),
            P(None, "dp", "expert"),
            gain_spec,
            rows_spec,
            rows_spec,
            rows_spec,
            P(),
            P(),
            rows_spec,
            gain_spec,
            rows_spec,
            expert_spec,
            expert_spec,
            expert_spec,
        ),
        out_specs=(
            token_spec,
            token_spec,
            gain_spec,
            rows_spec,
            rows_spec,
            rows_spec,
            P(),
            P(),
            rows_spec,
            gain_spec,
            rows_spec,
            expert_spec,
            expert_spec,
            expert_spec,
        ),
        check_vma=False,
    )
```

time: 5050 us -> 702 us (0.14)
  waiting for transfers between devices: 3980 us -> 235 us
  blocking collectives: 637 us -> 18.2 us
    reduce_scatter x7 -> x0, waiting for transfers between devices: 2770 us -> none  [the longest x1 642 us: body(): lax.psum_scatter(acc_out, ('dp', 'expert'), scatter_dimension=0, tiled=True)]
    all_gather x7 -> x3, waiting for transfers between devices: 1110 us -> 26.2 us  [the longest x1 26.1 us: body(): dense = lax.all_gather(packed, 'dp', axis=0, tiled=True)]
    all_gather x1 -> x0, blocking collectives: 342 us -> none  [fetch_all(): lax.all_gather(w_router, ('dp', 'expert'), axis=0, tiled=True)]
    unnamed x2 -> x0, blocking collectives: 156 us -> none
    all_to_all x5 -> x11, waiting for transfers between devices: 57.1 us -> 205 us  [the longest x3 82.4 us: spread(): lax.all_to_all(jnp.broadcast_to(values[None], (count,) + values.shape), a...]
    all_to_all x3 -> x1, blocking collectives: 139 us -> 18.2 us  [spread(): lax.all_to_all(jnp.broadcast_to(values[None], (count,) + values.shape), a...]
    dot_general x40 -> x20, matrix products: 95.1 us -> 114 us  [the longest x17 107 us: einsum(): return jnp.einsum(spec, left_side, right_side, preferred_element_type=f32)]
  transfers between devices with their start and end apart: 36 -> 22, of which waited for: 26 -> 10; matrix products, arithmetic and copies ran while one was open for 3% -> 45% of each run, Pallas kernels for 0% -> 0%
where the time goes in v1:
time: 702 us; the launch traced here: 694 us
  waiting for transfers between devices  235 us (33%)
  matrix products  137 us (20%)
  local copies, waits for them, and re-layouts  129 us (18%)
  other arithmetic  83.9 us (12%)
  starting transfers between devices  75.3 us (11%)
  blocking collectives  18.2 us (3%)
  between operations  15.4 us (2%)
    dot_general x17, matrix products, einsum(): return jnp.einsum(spec, left_side, right_side, preferred_element_type=f32)  107 us
    all_to_all x3, waiting for transfers between devices, spread(): lax.all_to_all(jnp.broadcast_to(values[None], (count,) + values.shape), a...  82.4 us
    all_to_all x4, waiting for transfers between devices, sum_to_owner(): arrived = lax.all_to_all(both, 'dp', 0, 0, axis_index_groups=groups)  72.8 us
    all_to_all x1, waiting for transfers between devices, body(): moe_back = lax.all_to_all(back_part, 'expert', 0, 0)  42.6 us
    all_gather x1, waiting for transfers between devices, body(): dense = lax.all_gather(packed, 'dp', axis=0, tiled=True)  26.1 us
    all_to_all x4, starting transfers between devices, sum_to_owner(): arrived = lax.all_to_all(both, 'dp', 0, 0, axis_index_groups=groups)  19.3 us
    all_to_all x1, blocking collectives, spread(): lax.all_to_all(jnp.broadcast_to(values[None], (count,) + values.shape), a...  18.2 us
    convert_element_type x4, other arithmetic, sum_to_owner(): both = (kept.astype(f32) + received.astype(f32)).astype(bf16)  17.3 us
  transfers between devices with their start and end apart: 22, of which 10 were waited for; matrix products, arithmetic and copies ran while one was open for 45% of the time, Pallas kernels for 0%

profile of v1, /device:TPU:0, one launch (start us, length us, event | category | flops | bytes accessed | tf_op | source)
XLA Modules:
  0.0 694.2 jit_solution(8022818169757705669)
XLA Ops:
  9.7 18.2 %all_to_all.60 = bf16[8,8,3200]{2,1,0:T(8,128)(2,1)} all-to-all(bf16[8,8,3200]{2,1,0:T(8,128)(2,1)S(1)} %broadcast_in_dim.75), channel_id=1, replica_groups=mesh['dp'=16,'expert'=8] {'expert'}, dimensions={0} | all-to-all | bytes 819200 | tf_op jit(solution)/shard_map/all_to_all | solution.py:72
  31.3 4.0 all-to-all-start.1
  42.9 26.1 %all-gather.4.cloned.1.call-done = bf16[1024,3200]{1,0:T(8,128)(2,1)} async-done(((bf16[64,3200]{1,0:T(8,128)(2,1)}), bf16[1024,3200]{1,0:T(8,128)(2,1)}) %all-gather.4.cloned.1.call-update) | async-done | bytes 6553616 | tf_op jit(solution)/shard_map/all_gather | solution.py:143
  70.7 3.6 fusion.19
  86.5 4.3 collective-permute-start
  90.7 5.7 collective-permute-start.1
  99.1 3.9 broadcast_in_dim.94
  103.0 4.9 all-to-all-start.4
  115.5 4.0 collective-permute-done.1
  121.7 6.1 fusion.123
  127.8 3.6 fusion.49
  131.9 2.6 multiply_reduce_fusion.4
  135.7 53.7 %all-to-all-done.4 = bf16[8,2,128,1024]{3,2,1,0:T(8,128)(2,1)} async-done(((bf16[8,2,128,1024]{3,2,1,0:T(8,128)(2,1)}), bf16[8,2,128,1024]{3,2,1,0:T(8,128)(2,1)}, u32[]{:S(2)}, u32[]{:S(2)}) %all-to-all-start.4) | async-done | bytes 4194336 | tf_op jit(solution)/shard_map/all_to_all | solution.py:72
  192.0 8.1 %all-to-all-start.2 = ((bf16[8,2,128,1024]{3,2,1,0:T(8,128)(2,1)}), bf16[8,2,128,1024]{3,2,1,0:T(8,128)(2,1)}, u32[]{:S(2)}, u32[]{:S(2)}) async-start(bf16[8,2,128,1024]{3,2,1,0:T(8,128)(2,1)} %broadcast_in_dim.87), calls=%async_computation.2 | async-start | bytes 8388608 | tf_op jit(solution)/shard_map/all_to_all | solution.py:72
  201.5 8.5 %convolution_bitcast_fusion = f32[4,16,48,1024]{3,2,0,1:T(8,128)} fusion(bf16[16,128,1024,1]{2,1,3,0:T(8,128)(2,1)} %bitcast.45, s32[16,4,128]{2,1,0:T(4,128)S(1)} %copy.313), kind=kOutput, calls=%fused_computation.37 | convolution fusion | flops 805699584 | bytes 16809984 | tf_op jit(solution)/shard_map/bjct,btd->jbcd/dot_general | solution.py:67
  210.0 11.8 %copy.319 = f32[4,16,48,1024]{3,2,1,0:T(8,128)} copy(f32[4,16,48,1024]{3,2,0,1:T(8,128)} %convolution_bitcast_fusion) | data formatting | bytes 25165824 | tf_op jit(solution)/shard_map/bjct,btd->jbcd/transpose | solution.py:67
  221.8 28.7 %all-to-all-done.2 = bf16[8,2,128,1024]{3,2,1,0:T(8,128)(2,1)} async-done(((bf16[8,2,128,1024]{3,2,1,0:T(8,128)(2,1)}), bf16[8,2,128,1024]{3,2,1,0:T(8,128)(2,1)}, u32[]{:S(2)}, u32[]{:S(2)}) %all-to-all-start.2) | async-done | bytes 4194336 | tf_op jit(solution)/shard_map/all_to_all | solution.py:72
  250.5 4.0 convert_bitcast_fusion
  254.5 3.3 copy.316
  257.8 10.0 %fusion.130 = f32[4,768,1024]{2,1,0:T(8,128)S(1)} fusion(bf16[4,768,1024]{2,1,0:T(8,128)(2,1)} %bitcast.325, bf16[4,1024,1024]{2,1,0:T(8,128)(2,1)} %all-gather.6.cloned.1.call-done), kind=kOutput, calls=%fused_computation.245 | convolution fusion | flops 6442450944 | bytes 27262976 | tf_op jit(solution)/shard_map/ecd,edf->ecf/dot_general | solution.py:67
  267.8 4.5 copy-done.5
  274.4 9.9 %fusion.2 = (f32[4,768]{1,0:T(4,128)S(1)}, bf16[4,768,1024]{2,1,0:T(8,128)(2,1)}) fusion(f32[4,16,48,1024]{3,2,1,0:T(8,128)} %copy.319, bf16[4,768,512]{2,1,0:T(8,128)(2,1)S(1)} %multiply_convert_fusion.2, bf16[4,512,1024]{2,1,0:T(8,128)(2,1)} %all-gather.8.cloned.1.call-done), kind=kOutput, calls=%fused_computation.4 | convolution fusion | flops 3233805312 | bytes 26226688 | tf_op jit(solution)/shard_map/ecf,efd->ecd/dot_general | solution.py:67
  284.4 3.6 fusion.128
  289.9 3.9 all-to-all-start.5
  293.7 10.1 %fusion.3 = (bf16[4,768,1024]{2,1,0:T(8,128)(2,1)S(1)}, bf16[4,768,1024]{2,1,0:T(8,128)(2,1)}) fusion(f32[4,16,48,1024]{3,2,1,0:T(8,128)} %copy.319, f32[4,768]{1,0:T(4,128)S(1)} %mul.609, bf16[4,768,1024]{2,1,0:T(8,128)(2,1)} %get-tuple-element.157), kind=kLoop, calls=%fused_computation.6 | loop fusion | flops 15728640 | bytes 31469568 | tf_op jit(solution)/shard_map/convert_element_type | solution.py:232
  303.8 13.3 %multiply_convert_fusion.1 = (bf16[4,768,512]{2,1,0:T(8,128)(2,1)}, bf16[4,768,512]{2,1,0:T(8,128)(2,1)}) fusion(f32[4,768,1024]{2,1,0:T(8,128)} %copy-done.5, bf16[4,768,1024]{2,1,0:T(8,128)(2,1)S(1)} %get-tuple-element.144, bf16[4,512,1024]{2,1,0:T(8,128)(2,1)} %all-gather.8.cloned.1.call-done), kind=kOutput, calls=%fused_computation.27 | convolution fusion | flops 3241672704 | bytes 29360128 | tf_op jit(solution)/shard_map/ecd,efd->ecf/dot_general | solution.py:67
  317.1 13.0 %fusion.21 = bf16[4,768,1024]{2,1,0:T(8,128)(2,1)} fusion(bf16[4,1024,1024]{2,1,0:T(8,128)(2,1)} %all-gather.6.cloned.1.call-done, bf16[4,768,512]{2,1,0:T(8,128)(2,1)} %get-tuple-element.109, bf16[4,768,512]{2,1,0:T(8,128)(2,1)} %get-tuple-element.108), kind=kOutput, calls=%fused_computation.51 | convolution fusion | flops 6458179584 | bytes 20971520 | tf_op jit(solution)/shard_map/ecf,edf->ecd/dot_general | solution.py:67
  330.1 6.1 bitcast_convert_fusion
  336.1 7.2 %all-to-all-start.6 = ((bf16[8,2,128,1024]{3,2,1,0:T(8,128)(2,1)}), bf16[8,2,128,1024]{3,2,1,0:T(8,128)(2,1)}, u32[]{:S(2)}, u32[]{:S(2)}) async-start(bf16[8,2,128,1024]{3,2,1,0:T(8,128)(2,1)} %bitcast.320), calls=%async_computation.6 | async-start | bytes 8388608 | tf_op jit(solution)/shard_map/all_to_all | solution.py:259
  343.4 6.1 bitcast_convert_fusion.1
  349.5 42.6 %all-to-all-done.6 = bf16[8,2,128,1024]{3,2,1,0:T(8,128)(2,1)} async-done(((bf16[8,2,128,1024]{3,2,1,0:T(8,128)(2,1)}), bf16[8,2,128,1024]{3,2,1,0:T(8,128)(2,1)}, u32[]{:S(2)}, u32[]{:S(2)}) %all-to-all-start.6) | async-done | bytes 4194336 | tf_op jit(solution)/shard_map/all_to_all | solution.py:259
  392.1 4.7 all-to-all-start.3
  396.8 6.5 convolution_convert_fusion.3
  414.6 12.7 %convolution_convert_fusion = bf16[4,1024,1024]{2,1,0:T(8,128)(2,1)} fusion(bf16[4,768,1024]{2,1,0:T(8,128)(2,1)} %bitcast.326, bf16[4,768,512]{2,1,0:T(8,128)(2,1)} %get-tuple-element.109, bf16[4,768,512]{2,1,0:T(8,128)(2,1)} %get-tuple-element.108), kind=kOutput, calls=%fused_computation.14 | convolution fusion | flops 6459228160 | bytes 20971520 | tf_op jit(solution)/shard_map/ecd,ecf->edf/dot_general | solution.py:67
  427.3 8.6 %copy.354 = bf16[4,16,64,1024]{3,2,0,1:T(8,128)(2,1)} copy(bf16[4,16,64,1024]{3,2,1,0:T(8,128)(2,1)} %bitcast.323) | data formatting | bytes 16777216 | tf_op jit(solution)/shard_map/reshape | solution.py:263
  436.2 3.9 fusion.15
  440.0 3.2 convert_reduce_fusion.1
  446.1 5.3 all-to-all-start.11
  451.4 3.2 convert_reduce_fusion.2
  457.8 3.3 fusion.46
  461.2 2.7 reshape.483
  465.9 4.4 fusion.5
  489.1 4.4 copy.376
  494.1 12.9 %concatenate.101 = bf16[1024,1152]{0,1:T(8,128)(2,1)} concatenate(bf16[1024,1024]{0,1:T(8,128)(2,1)} %convolution_convert_fusion.4, bf16[1024,32]{0,1:T(8,128)(2,1)S(1)} %convolution_convert_fusion.5, bf16[1024,1]{0,1:T(2,128)(2,1)} %broadcast_in_dim.96, bf16[1024,95]{0,1:T(8,128)(2,1)S(1)} %broadcast_in_dim.97), dimensions={1} | concatenate | bytes 4718592 | tf_op jit(solution)/shard_map/concatenate | solution.py:288
  507.0 4.4 copy.349
  514.9 2.5 copy.333
  517.5 4.1 reshape.482
  521.6 4.8 multiply_reduce_fusion
  535.4 4.6 convolution_convert_fusion.1
  540.1 4.6 fusion.68
  545.1 2.7 pad_maximum_fusion.1
  548.2 3.7 copy-done.13
  556.4 5.7 all-to-all-start.7
  562.1 4.2 fusion.14
  566.4 13.1 %all-to-all-done.7 = bf16[8,64,1152]{2,1,0:T(8,128)(2,1)S(1)} async-done(((bf16[8,64,1152]{2,1,0:T(8,128)(2,1)}), bf16[8,64,1152]{2,1,0:T(8,128)(2,1)S(1)}, u32[]{:S(2)}, u32[]{:S(2)}) %all-to-all-start.7) | async-done | bytes 1179680 | tf_op jit(solution)/shard_map/all_to_all | solution.py:91
  580.5 3.8 all-to-all-start.8
  584.3 7.9 %fusion.4 = bf16[8,4,64,1024]{3,2,1,0:T(8,128)(2,1)} fusion(bf16[8,4,64,1024]{3,2,1,0:T(8,128)(2,1)} %collective-permute-done.6, bf16[8,2,4,64,1024]{4,3,2,1,0:T(8,128)(2,1)} %bitcast.310, s32[]{:T(128)S(6)} %select_n.77), kind=kLoop, calls=%fused_computation.8 | loop fusion | flops 8388608 | bytes 12582916 | tf_op jit(solution)/shard_map/convert_element_type | solution.py:89
  592.2 19.8 %all-to-all-done.8 = bf16[8,64,2176]{2,1,0:T(8,128)(2,1)S(1)} async-done(((bf16[8,64,2176]{2,1,0:T(8,128)(2,1)}), bf16[8,64,2176]{2,1,0:T(8,128)(2,1)S(1)}, u32[]{:S(2)}, u32[]{:S(2)}) %all-to-all-start.8) | async-done | bytes 2228256 | tf_op jit(solution)/shard_map/all_to_all | solution.py:91
  611.9 4.6 all-to-all-start.10
  616.5 2.8 convert_reduce_fusion.3
  624.4 40.0 %all-to-all-done.10 = bf16[8,4,64,1024]{3,2,1,0:T(8,128)(2,1)} async-done(((bf16[8,4,64,1024]{3,2,1,0:T(8,128)(2,1)}), bf16[8,4,64,1024]{3,2,1,0:T(8,128)(2,1)}, u32[]{:S(2)}, u32[]{:S(2)}) %all-to-all-start.10) | async-done | bytes 4194336 | tf_op jit(solution)/shard_map/all_to_all | solution.py:91
  664.4 9.7 %all-to-all-start.9 = ((bf16[8,8,3328]{2,1,0:T(8,128)(2,1)}), bf16[8,8,3328]{2,1,0:T(8,128)(2,1)S(1)}, u32[]{:S(2)}, u32[]{:S(2)}) async-start(bf16[8,8,3328]{2,1,0:T(8,128)(2,1)} %pad_maximum_fusion.14), calls=%async_computation.9 | async-start | bytes 851968 | tf_op jit(solution)/shard_map/all_to_all | solution.py:360
  674.1 3.2 convert_reduce_fusion
  678.3 5.4 all-to-all-done.9
  (329 shorter events, 115.9 us)
Async XLA Ops:
  7.2 30.1 %copy-start.22 = (bf16[2,1,128,1024]{3,2,1,0:T(8,128)(2,1)S(1)}, bf16[2,1,128,1024]{3,2,1,0:T(8,128)(2,1)}, u32[]{:S(2)}) copy-start(bf16[2,1,128,1024]{3,2,1,0:T(8,128)(2,1)} %param.17) | copy-start | bytes 1572868
  7.2 30.3 %copy-start.65 = (bf16[64]{0:T(256)(128)(2,1)S(1)}, bf16[64]{0:T(256)(128)(2,1)}, u32[]{:S(2)}) copy-start(bf16[64]{0:T(256)(128)(2,1)} %param.27) | copy-start | bytes 388
  7.2 32.8 %copy-start.66 = (bf16[64]{0:T(256)(128)(2,1)S(1)}, bf16[64]{0:T(256)(128)(2,1)}, u32[]{:S(2)}) copy-start(bf16[64]{0:T(256)(128)(2,1)} %param.26) | copy-start | bytes 388
  7.2 33.9 %copy-start.63 = (s32[2,1,128]{2,1,0:T(1,128)S(1)}, s32[2,1,128]{2,1,0:T(1,128)}, u32[]{:S(2)}) copy-start(s32[2,1,128]{2,1,0:T(1,128)} %param.21) | copy-start | bytes 3076
  7.2 33.9 %copy-start.34 = (bf16[2,1,128,1024]{3,2,1,0:T(8,128)(2,1)S(1)}, bf16[2,1,128,1024]{3,2,1,0:T(8,128)(2,1)}, u32[]{:S(2)}) copy-start(bf16[2,1,128,1024]{3,2,1,0:T(8,128)(2,1)} %param.18) | copy-start | bytes 1572868
  7.2 61.9 %all-gather.4.cloned.1.call-start = ((), (), s32[]{:S(2)}) async-start(), calls=%async_computation.12 | async-start | bytes 6963200 | tf_op jit(solution)/shard_map/all_gather | solution.py:143
  28.0 229.8 %all-gather.6.cloned.1.call-start = ((), (), s32[]{:S(2)}) async-start(), calls=%async_computation.13 | async-start | bytes 8912896 | tf_op jit(solution)/shard_map/all_gather | solution.py:149
  31.3 67.9 %all-to-all-start.1 = ((s32[8,2,128,8]{2,3,1,0:T(8,128)}), s32[8,2,128,8]{2,3,1,0:T(8,128)}, u32[]{:S(2)}, u32[]{:S(2)}) async-start(s32[8,2,128,8]{2,3,1,0:T(8,128)} %broadcast_in_dim.84), calls=%async_computation.1 | async-start | bytes 131072 | tf_op jit(solution)/shard_map/all_to_all | solution.py:72
  35.2 239.1 %all-gather.8.cloned.1.call-start = ((), (), s32[]{:S(2)}) async-start(), calls=%async_computation.14 | async-start | bytes 4456448 | tf_op jit(solution)/shard_map/all_gather | solution.py:152
  37.5 36.9 %copy-start.56 = (f32[256]{0:T(256)}, f32[256]{0:T(256)S(1)}, u32[]{:S(2)}) copy-start(f32[256]{0:T(256)S(1)} %rsqrt_bitcast_fusion) | copy-start | bytes 3076
  38.2 40.1 %copy-start.39 = (f32[256,64]{0,1:T(8,128)}, f32[256,64]{0,1:T(8,128)S(1)}, u32[]{:S(2)}) copy-start(f32[256,64]{0,1:T(8,128)S(1)} %pad_maximum_fusion.16) | copy-start | bytes 196612
  40.0 44.0 %copy-start.53 = (f32[512]{0:T(512)}, f32[512]{0:T(512)S(1)}, u32[]{:S(2)}) copy-start(f32[512]{0:T(512)S(1)} %mul.567) | copy-start | bytes 6148
  70.7 4.6 copy-start.45
  74.4 22.0 %copy-start.18 = (f32[256,2048]{1,0:T(8,128)}, f32[256,2048]{1,0:T(8,128)S(1)}, u32[]{:S(2)}) copy-start(f32[256,2048]{1,0:T(8,128)S(1)} %fusion.19) | copy-start | bytes 6291460
  76.6 8.9 %copy-start.14 = (f32[256,512]{0,1:T(8,128)}, f32[256,512]{0,1:T(8,128)S(1)}, u32[]{:S(2)}) copy-start(f32[256,512]{0,1:T(8,128)S(1)} %copy.299) | copy-start | bytes 1572868
  85.6 10.9 %copy-start.30 = (bf16[256,512]{1,0:T(8,128)(2,1)}, bf16[256,512]{1,0:T(8,128)(2,1)S(1)}, u32[]{:S(2)}) copy-start(bf16[256,512]{1,0:T(8,128)(2,1)S(1)} %add_convert_fusion) | copy-start | bytes 786436
  86.5 29.0 %collective-permute-start = (bf16[2,128,1024]{2,1,0:T(8,128)(2,1)}, bf16[2,128,1024]{2,1,0:T(8,128)(2,1)}, u32[]{:S(2)}, u32[]{:S(2)}) collective-permute-start(bf16[2,128,1024]{2,1,0:T(8,128)(2,1)} %pad_maximum_fusion.9), channel_id=1, source_target_pairs={{0,2},{1,3},{2,4},{3,5},{4,6},{5,7},{8,10},{9,11},{10,12},{11,13},... | collective-permute-start | bytes 1572872 | tf_op jit(solution)/shard_map/ppermute | solution.py:78
  90.7 28.7 %collective-permute-start.1 = (bf16[2,128,1024]{2,1,0:T(8,128)(2,1)}, bf16[2,128,1024]{2,1,0:T(8,128)(2,1)}, u32[]{:S(2)}, u32[]{:S(2)}) collective-permute-start(bf16[2,128,1024]{2,1,0:T(8,128)(2,1)} %pad_maximum_fusion.9), channel_id=1, source_target_pairs={{0,1},{1,2},{2,3},{3,4},{4,5},{5,6},{6,7},{8,9},{9,10},{10,11},{11... | collective-permute-start | bytes 1572872 | tf_op jit(solution)/shard_map/ppermute | solution.py:78
  99.1 10.5 %copy-start = (f32[256,1024]{0,1:T(8,128)}, f32[256,1024]{0,1:T(8,128)S(1)}, u32[]{:S(2)}) copy-start(f32[256,1024]{0,1:T(8,128)S(1)} %copy.307) | copy-start | bytes 3145732
  103.0 6.6 copy-start.60
  103.0 86.4 %all-to-all-start.4 = ((bf16[8,2,128,1024]{3,2,1,0:T(8,128)(2,1)}), bf16[8,2,128,1024]{3,2,1,0:T(8,128)(2,1)}, u32[]{:S(2)}, u32[]{:S(2)}) async-start(bf16[8,2,128,1024]{3,2,1,0:T(8,128)(2,1)} %broadcast_in_dim.94), calls=%async_computation.4 | async-start | bytes 8388608 | tf_op jit(solution)/shard_map/all_to_all | solution.py:72
  108.1 5.5 copy-start.46
  108.1 5.5 copy-start.47
  109.7 9.8 %copy-start.31 = (bf16[256,512]{1,0:T(8,128)(2,1)S(1)}, bf16[256,512]{1,0:T(8,128)(2,1)}, u32[]{:S(2)}) copy-start(bf16[256,512]{1,0:T(8,128)(2,1)} %copy-done.30) | copy-start | bytes 786436
  115.5 6.2 copy-start.49
  121.3 6.5 copy-start.28
  121.7 6.1 copy-start.42
  135.7 56.3 %copy-start.16 = (bf16[256,1024]{1,0:T(8,128)(2,1)}, bf16[256,1024]{1,0:T(8,128)(2,1)S(1)}, u32[]{:S(2)}) copy-start(bf16[256,1024]{1,0:T(8,128)(2,1)S(1)} %multiply_convert_fusion.3) | copy-start | bytes 1572868
  192.0 58.5 %all-to-all-start.2 = ((bf16[8,2,128,1024]{3,2,1,0:T(8,128)(2,1)}), bf16[8,2,128,1024]{3,2,1,0:T(8,128)(2,1)}, u32[]{:S(2)}, u32[]{:S(2)}) async-start(bf16[8,2,128,1024]{3,2,1,0:T(8,128)(2,1)} %broadcast_in_dim.87), calls=%async_computation.2 | async-start | bytes 8388608 | tf_op jit(solution)/shard_map/all_to_all | solution.py:72
  289.9 46.3 %all-to-all-start.5 = ((f32[8,2,4,128]{3,1,2,0:T(2,128)}), f32[8,2,4,128]{3,1,2,0:T(2,128)S(1)}, u32[]{:S(2)}, u32[]{:S(2)}) async-start(f32[8,2,4,128]{3,1,2,0:T(2,128)} %copy.322), calls=%async_computation.5 | async-start | bytes 65536 | tf_op jit(solution)/shard_map/all_to_all | solution.py:258
  303.8 13.3 %copy-start.19 = (bf16[4,768,1024]{2,1,0:T(8,128)(2,1)}, bf16[4,768,1024]{2,1,0:T(8,128)(2,1)S(1)}, u32[]{:S(2)}) copy-start(bf16[4,768,1024]{2,1,0:T(8,128)(2,1)S(1)} %get-tuple-element.144) | copy-start | bytes 18874372
  336.1 55.9 %all-to-all-start.6 = ((bf16[8,2,128,1024]{3,2,1,0:T(8,128)(2,1)}), bf16[8,2,128,1024]{3,2,1,0:T(8,128)(2,1)}, u32[]{:S(2)}, u32[]{:S(2)}) async-start(bf16[8,2,128,1024]{3,2,1,0:T(8,128)(2,1)} %bitcast.320), calls=%async_computation.6 | async-start | bytes 8388608 | tf_op jit(solution)/shard_map/all_to_all | solution.py:259
  392.1 54.1 %all-to-all-start.3 = ((bf16[8,2,128,1024]{3,2,1,0:T(8,128)(2,1)}), bf16[8,2,128,1024]{3,2,1,0:T(8,128)(2,1)}, u32[]{:S(2)}, u32[]{:S(2)}) async-start(bf16[8,2,128,1024]{3,2,1,0:T(8,128)(2,1)} %bitcast.319), calls=%async_computation.3 | async-start | bytes 8388608 | tf_op jit(solution)/shard_map/all_to_all | solution.py:260
  403.8 4.9 copy-start.67
  403.8 5.6 copy-start.64
  407.3 28.9 %collective-permute-start.7 = (bf16[8,4,32,1024]{3,2,1,0:T(8,128)(2,1)}, bf16[8,4,32,1024]{3,2,1,0:T(8,128)(2,1)}, u32[]{:S(2)}, u32[]{:S(2)}) collective-permute-start(bf16[8,4,32,1024]{3,2,1,0:T(8,128)(2,1)} %dynamic-slice_bitcast_fusion.2), channel_id=1, source_target_pairs={{0,8},{8,0},{16,24},{24,16},{32,40},{40,32},{48,56},{56,48},{64,72... | collective-permute-start | bytes 6291464 | tf_op jit(solution)/shard_map/ppermute | solution.py:88
  407.4 4.9 copy-start.52
  427.3 8.9 %copy-start.4 = (bf16[4,16,32,1024]{3,2,0,1:T(8,128)(2,1)S(1)}, bf16[4,16,32,1024]{3,2,0,1:T(8,128)(2,1)}, u32[]{:S(2)}) copy-start(bf16[4,16,32,1024]{3,2,0,1:T(8,128)(2,1)} %copy-done.3) | copy-start | bytes 12582916
  444.8 9.8 %copy-start.35 = (bf16[2,1,128,1024]{3,2,1,0:T(8,128)(2,1)S(1)}, bf16[2,1,128,1024]{3,2,1,0:T(8,128)(2,1)}, u32[]{:S(2)}) copy-start(bf16[2,1,128,1024]{3,2,1,0:T(8,128)(2,1)} %param.18) | copy-start | bytes 1572868
  446.1 110.3 %all-to-all-start.11 = ((bf16[8,4,32,1024]{3,2,1,0:T(8,128)(2,1)}), bf16[8,4,32,1024]{3,2,1,0:T(8,128)(2,1)}, u32[]{:S(2)}, u32[]{:S(2)}) async-start(bf16[8,4,32,1024]{3,2,1,0:T(8,128)(2,1)} %fusion.15), calls=%async_computation.11 | async-start | bytes 4194304 | tf_op jit(solution)/shard_map/all_to_all | solution.py:91
  457.8 12.5 %slice-start.2 = ((s8[6291456]{0:T(1024)(128)(4,1)}), s8[2097152]{0:T(1024)(128)(4,1)S(1)}, s32[]{:S(2)}) async-start(s8[6291456]{0:T(1024)(128)(4,1)} %bitcast.329), calls=%async_computation.17 | async-start | bytes 4194304
  485.1 41.4 %collective-permute-start.2 = (bf16[2,128,1024]{2,1,0:T(8,128)(2,1)}, bf16[2,128,1024]{2,1,0:T(8,128)(2,1)}, u32[]{:S(2)}, u32[]{:S(2)}) collective-permute-start(bf16[2,128,1024]{2,1,0:T(8,128)(2,1)} %get-tuple-element.114), channel_id=1, source_target_pairs={{1,0},{2,1},{3,2},{4,3},{5,4},{6,5},{7,6},{9,8},{10,9},{11,10},{12... | collective-permute-start | bytes 1572872 | tf_op jit(solution)/shard_map/ppermute | solution.py:78
  486.5 40.0 %collective-permute-start.3 = (bf16[2,128,1024]{2,1,0:T(8,128)(2,1)}, bf16[2,128,1024]{2,1,0:T(8,128)(2,1)}, u32[]{:S(2)}, u32[]{:S(2)}) collective-permute-start(bf16[2,128,1024]{2,1,0:T(8,128)(2,1)} %get-tuple-element.115), channel_id=1, source_target_pairs={{2,0},{3,1},{4,2},{5,3},{6,4},{7,5},{10,8},{11,9},{12,10},{13,11},... | collective-permute-start | bytes 1572872 | tf_op jit(solution)/shard_map/ppermute | solution.py:78
  511.3 10.2 %copy-start.55 = (f32[1024]{0:T(1024)S(1)}, f32[1024]{0:T(1024)}, u32[]{:S(2)}) copy-start(f32[1024]{0:T(1024)} %mul.647) | copy-start | bytes 12292
  526.5 4.8 copy-start.62
  529.1 4.6 copy-start.26
  529.1 4.6 copy-start.54
  535.3 4.8 copy-start.23
  535.3 4.8 copy-start.43
  535.3 4.8 copy-start.48
  535.3 4.8 copy-start.51
  535.3 4.8 copy-start.57
  545.1 7.0 %slice-start = ((s8[8388608]{0:T(1024)(128)(4,1)}), s8[4194304]{0:T(1024)(128)(4,1)S(1)}, s32[]{:S(2)}) async-start(s8[8388608]{0:T(1024)(128)(4,1)} %bitcast.311), calls=%async_computation.15 | async-start | bytes 8388608
  545.1 7.0 %slice-start.1 = ((s8[8388608]{0:T(1024)(128)(4,1)}), s8[4194304]{0:T(1024)(128)(4,1)S(1)}, s32[]{:S(2)}) async-start(s8[8388608]{0:T(1024)(128)(4,1)} %bitcast.311), calls=%async_computation.16 | async-start | bytes 8388608
  547.9 6.8 copy-start.2
  548.1 14.0 %collective-permute-start.5 = (bf16[8,64,2176]{2,1,0:T(8,128)(2,1)S(1)}, bf16[8,64,2176]{2,1,0:T(8,128)(2,1)}, u32[]{:S(2)}, u32[]{:S(2)}) collective-permute-start(bf16[8,64,2176]{2,1,0:T(8,128)(2,1)S(1)} %dynamic-slice_bitcast_fusion.1), channel_id=1, source_target_pairs={{0,8},{8,0},{16,24},{24,16},{32,40},{40,32},{48,56},{56,48},{64,72... | collective-permute-start | bytes 6684680 | tf_op jit(solution)/shard_map/ppermute | solution.py:88
  552.0 3.1 collective-permute-start.4
  554.6 29.7 %collective-permute-start.6 = (bf16[8,4,64,1024]{3,2,1,0:T(8,128)(2,1)}, bf16[8,4,64,1024]{3,2,1,0:T(8,128)(2,1)}, u32[]{:S(2)}, u32[]{:S(2)}) collective-permute-start(bf16[8,4,64,1024]{3,2,1,0:T(8,128)(2,1)} %dynamic-slice_bitcast_fusion), channel_id=1, source_target_pairs={{0,8},{8,0},{16,24},{24,16},{32,40},{40,32},{48,56},{56,48},{64,72... | collective-permute-start | bytes 12582920 | tf_op jit(solution)/shard_map/ppermute | solution.py:88
  556.4 23.1 %all-to-all-start.7 = ((bf16[8,64,1152]{2,1,0:T(8,128)(2,1)}), bf16[8,64,1152]{2,1,0:T(8,128)(2,1)S(1)}, u32[]{:S(2)}, u32[]{:S(2)}) async-start(bf16[8,64,1152]{2,1,0:T(8,128)(2,1)} %fusion.30), calls=%async_computation.7 | async-start | bytes 2359296 | tf_op jit(solution)/shard_map/all_to_all | solution.py:91
  580.5 31.4 %all-to-all-start.8 = ((bf16[8,64,2176]{2,1,0:T(8,128)(2,1)}), bf16[8,64,2176]{2,1,0:T(8,128)(2,1)S(1)}, u32[]{:S(2)}, u32[]{:S(2)}) async-start(bf16[8,64,2176]{2,1,0:T(8,128)(2,1)} %fusion.14), calls=%async_computation.8 | async-start | bytes 4456448 | tf_op jit(solution)/shard_map/all_to_all | solution.py:91
  592.2 24.3 %copy-start.59 = (f32[2,128]{1,0:T(2,128)S(1)}, f32[2,128]{1,0:T(2,128)}, u32[]{:S(2)}) copy-start(f32[2,128]{1,0:T(2,128)} %copy-done.58) | copy-start | bytes 3076
  592.2 27.2 %copy-start.7 = (f32[256,1024]{1,0:T(8,128)S(1)}, f32[256,1024]{1,0:T(8,128)}, u32[]{:S(2)}) copy-start(f32[256,1024]{1,0:T(8,128)} %copy-done.6) | copy-start | bytes 3145732
  611.9 52.4 %all-to-all-start.10 = ((bf16[8,4,64,1024]{3,2,1,0:T(8,128)(2,1)}), bf16[8,4,64,1024]{3,2,1,0:T(8,128)(2,1)}, u32[]{:S(2)}, u32[]{:S(2)}) async-start(bf16[8,4,64,1024]{3,2,1,0:T(8,128)(2,1)} %fusion.4), calls=%async_computation.10 | async-start | bytes 8388608 | tf_op jit(solution)/shard_map/all_to_all | solution.py:91
  664.4 19.4 %all-to-all-start.9 = ((bf16[8,8,3328]{2,1,0:T(8,128)(2,1)}), bf16[8,8,3328]{2,1,0:T(8,128)(2,1)S(1)}, u32[]{:S(2)}, u32[]{:S(2)}) async-start(bf16[8,8,3328]{2,1,0:T(8,128)(2,1)} %pad_maximum_fusion.14), calls=%async_computation.9 | async-start | bytes 851968 | tf_op jit(solution)/shard_map/all_to_all | solution.py:360
  (30 other events, 92.0 us)
Sparse Core Ops, SparseCore 0:
  28.1 40.9 all-gather.3
  70.7 78.5 all-gather.5
  151.0 50.0 all-gather.7
